TPU v7x, 32 devices: a whole 2x2x4 slice. The times are simulated.
32 devices in a mesh: groups: 2 (over y), sketch: 4 (over z), context: 2 (over x), example: 2 (over core).
Axes of the slice: x: 2, y: 2, z: 4, core: 2. Of those that a mesh axis runs over, the one named last changes fastest.
Arguments:
- activations: bfloat16 [8, 4096, 512], P('groups', ('sketch', 'context')), parts along dimension 0, may hold values from -6 to 6
- out_grads: bfloat16 [8, 4096, 512], P('groups', ('sketch', 'example')), parts along dimension 0, may hold values from -6 to 6
- sign_bits: int32 [4, 2, 512, 2, 128], P(None, 'context', None, 'example'), may hold values from 0 to 65535
- keep_cols: int32 [128], replicated, may hold values from 0 to 31
- row_start: int32 [128], P(('context', 'example')), may hold values from 0 to 4095
- row_step: int32 [128], P(('context', 'example')), may hold values from 0 to 2047
- val_sketch: float32 [64, 8192], P('sketch', ('context', 'example')), may hold values from -6 to 6
Outputs:
- scores: float32 [8, 64], P(('groups', 'sketch')), parts along dimension 0
There are 2 independent parts, one for each index of `groups`. A program takes and returns all parts, laid end to end along the dimension named above; an argument that names none is the same for every part. Nothing has to cross between parts.
Inputs may be any that keep to these rules, and one draw needn't show every extreme that they name: `sign_bits`: each word holds 16 independent fair sign bits in its low 16 bits.
All inputs are finite; a program needn't handle non-finite values.
Results may differ from a plain program's by a relative error of at most 0.0003.
Values may be sent and summed in bfloat16 or wider, within the bound.
A program may use at most 128 MiB of HBM per device.

v0:
```python
import math

import jax
import jax.numpy as jnp
from jax import lax
from jax.sharding import PartitionSpec as P

KR = 64


def parity_sign(common, length):
    ones_total = jnp.zeros(common.shape, jnp.int32)
    for bit_place in range(max(length.bit_length() - 1, 1)):
        ones_total = ones_total + jnp.bitwise_and(jnp.right_shift(common, bit_place), 1)
    return (1 - 2 * jnp.bitwise_and(ones_total, 1)).astype(jnp.float32)


def hadamard_table(length):
    positions = jnp.arange(length, dtype=jnp.int32)
    common = jnp.bitwise_and(positions[:, None], positions[None, :])
    return parity_sign(common, length)


def hadamard_last(values):
    length = values.shape[-1]
    inner_len = min(128, length)
    outer_len = length // inner_len
    leading = values.shape[:-1]
    blocks = values.reshape(leading + (outer_len, inner_len))
    blocks = jnp.einsum(
        "...ab,bc->...ac", blocks, hadamard_table(inner_len), precision=lax.Precision.HIGHEST
    )
    blocks = jnp.einsum(
        "...ab,ac->...cb", blocks, hadamard_table(outer_len), precision=lax.Precision.HIGHEST
    )
    return blocks.reshape(values.shape) * (1.0 / math.sqrt(length))


def sign_table(packed):
    places = jnp.arange(16, dtype=jnp.int32)
    bit_values = jnp.bitwise_and(jnp.right_shift(packed[..., None], places), 1)
    return (
        (1 - 2 * bit_values)
        .astype(jnp.float32)
        .reshape(packed.shape[:-1] + (packed.shape[-1] * 16,))
    )


def body(activations, out_grads, sign_bits, keep_cols, row_start, row_step, val_sketch):
    sketch_count = lax.axis_size("sketch")
    context_count = lax.axis_size("context")
    example_count = lax.axis_size("example")
    example_index = lax.axis_index("example")
    feature_piece = activations.shape[1]
    column_piece = out_grads.shape[1]
    in_width = feature_piece * sketch_count * context_count
    out_width = column_piece * sketch_count * example_count
    local_width = column_piece * sketch_count
    kept_count = keep_cols.shape[0]
    block_width = out_width // kept_count
    columns = jnp.arange(kept_count, dtype=jnp.int32) * block_width + keep_cols
    arrived_in, arrived_out = (
        lax.all_to_all(activations, "sketch", split_axis=0, concat_axis=1, tiled=True),
        lax.all_to_all(out_grads, "sketch", split_axis=0, concat_axis=1, tiled=True),
    )
    gradient = jnp.einsum(
        "edt,ekt->dk", arrived_in, arrived_out, preferred_element_type=jnp.float32
    )
    words = sign_bits.reshape(sketch_count * feature_piece, -1)
    signed = gradient * sign_table(words)
    positions = jnp.arange(local_width, dtype=jnp.int32)
    global_cols = (
        positions // column_piece * example_count + example_index
    ) * column_piece + positions % column_piece
    common = jnp.bitwise_and(global_cols[:, None], columns[None, :])
    col_table = parity_sign(common, out_width) * (1.0 / math.sqrt(out_width))
    partial_value = jnp.dot(signed, col_table, precision=lax.Precision.HIGHEST)
    rows_local = signed.shape[0]
    per_device = kept_count // (context_count * example_count)
    split_cols = partial_value.reshape(rows_local, context_count, example_count, per_device)
    moved_parts = lax.all_to_all(split_cols, "context", split_axis=1, concat_axis=0, tiled=True)
    whole_rows = lax.psum_scatter(moved_parts, "example", scatter_dimension=2, tiled=True)
    ordered = whole_rows.reshape(context_count, sketch_count, feature_piece, per_device)
    ordered = jnp.transpose(ordered, (1, 0, 2, 3)).reshape(in_width, per_device)
    column = hadamard_last(ordered.T)
    strides = 2 * row_step + 1
    kept_rows = (
        row_start[:, None] + jnp.arange(KR, dtype=jnp.int32)[None, :] * strides[:, None]
    ) % in_width
    own_sketch = jnp.take_along_axis(column, kept_rows, axis=1).reshape(1, -1)
    products = jnp.dot(
        own_sketch,
        lax.all_gather(val_sketch, "sketch", axis=0, tiled=True).T,
        precision=lax.Precision.HIGHEST,
    )
    squares = jnp.sum(own_sketch * own_sketch, axis=1)
    products, squares = lax.psum((products, squares), ("context", "example"))
    return products / jnp.sqrt(squares + 1e-06)[:, None]


def solution(mesh):
    placed = (
        P("groups", ("sketch", "context"), None),
        P("groups", ("sketch", "example"), None),
        P(None, "context", None, "example", None),
        P(),
        P(("context", "example")),
        P(("context", "example")),
        P("sketch", ("context", "example")),
    )
    return jax.shard_map(
        body, mesh=mesh, in_specs=placed, out_specs=P(("groups", "sketch"), None), check_vma=False
    )
```

profile of v0, /device:TPU:0, one launch (start us, length us, event | category | flops | bytes accessed | tf_op | source)
XLA Modules:
  0.0 217.9 jit_solution(18444826817964610162)
XLA Ops:
  6.5 54.5 %all_to_all.36 = bf16[4,512,512]{2,1,0:T(8,128)(2,1)S(1)} all-to-all(bf16[4,512,512]{2,1,0:T(8,128)(2,1)} %param.7), channel_id=1, replica_groups=mesh['groups'=2,'sketch'=4,'context'=2,'example'=2] {'sketch'}, dimensions={0} | all-to-all | bytes 4194304 | tf_op jit(solution)/shard_map/all_to_all | solution.py:63
  61.0 4.5 %all-to-all-start.1 = ((bf16[4,512,512]{2,1,0:T(8,128)(2,1)}), bf16[4,512,512]{2,1,0:T(8,128)(2,1)}, u32[]{:S(2)}, u32[]{:S(2)}) async-start(bf16[4,512,512]{2,1,0:T(8,128)(2,1)} %param.8), calls=%async_computation.1 | async-start | bytes 4194304 | tf_op jit(solution)/shard_map/all_to_all | solution.py:64
  65.5 0.0 reduce-scatter.2.cloned.1.call-start
  65.6 1.6 copy.15
  67.1 7.9 %shift_right_arithmetic.157 = s32[2048,128,16]{0,2,1:T(8,128)} broadcast(s32[2048,128]{0,1:T(8,128)S(1)} %copy.15), dimensions={0,1} | broadcast | bytes 17825792 | tf_op jit(solution)/shard_map/shift_right_arithmetic | solution.py:41
  75.0 0.0 copy-start.2
  75.0 17.6 %copy.16 = s32[2048,2048]{1,0:T(8,128)} copy(s32[2048,2048]{0,1:T(8,128)} %bitcast.52) | data formatting | bytes 33554432 | tf_op jit(solution)/shard_map/shift_right_arithmetic | solution.py:41
  92.6 0.1 shift_right_arithmetic.160
  92.7 0.0 copy-done.2
  92.7 20.2 %all-to-all-done.1 = bf16[4,512,512]{2,1,0:T(8,128)(2,1)} async-done(((bf16[4,512,512]{2,1,0:T(8,128)(2,1)}), bf16[4,512,512]{2,1,0:T(8,128)(2,1)}, u32[]{:S(2)}, u32[]{:S(2)}) %all-to-all-start.1) | async-done | bytes 2097184 | tf_op jit(solution)/shard_map/all_to_all | solution.py:64
  112.9 0.0 slice-start
  112.9 0.0 slice-start.1
  112.9 0.0 slice-start.2
  112.9 0.0 slice-start.3
  112.9 11.0 %fusion.160 = f32[2048,2048]{1,0:T(8,128)} fusion(bf16[2048,512]{1,0:T(8,128)(2,1)S(1)} %bitcast.56, bf16[2048,512]{1,0:T(8,128)(2,1)} %bitcast.2), kind=kOutput, calls=%fused_computation.195 | convolution fusion | flops 4294967296 | bytes 20971520 | tf_op jit(solution)/shard_map/edt,ekt->dk/dot_general | solution.py:66
  124.0 0.0 slice-done
  124.0 0.0 slice-done.1
  124.0 0.0 slice-done.2
  124.0 0.0 slice-done.3
  124.0 0.0 copy-start.3
  124.0 0.0 copy-start.1
  124.0 0.0 copy-start
  124.0 25.7 %fusion = f32[2048,128]{0,1:T(8,128)S(1)} fusion(f32[2048,2048]{1,0:T(8,128)} %fusion.160, s32[2048,2048]{1,0:T(8,128)S(1)} %bitcast.51, s32[2048]{0:T(1024)S(1)} %shift_right_arithmetic.160, s32[128]{0:T(128)S(1)} %multiply_add_fusion, s32[2048]{0:T(1024)S(1)} %fusion.128), kind=kOutput, calls=%fused_computation.1 | convolution fusion | flops 6478364672 | bytes 34619904 | tf_op jit(solution)/shard_map/dot_general | solution.py:77
  149.8 15.5 %all_to_all.37 = f32[2048,2,2,32]{0,3,2,1:T(8,128)S(1)} all-to-all(f32[2048,2,2,32]{0,3,2,1:T(8,128)S(1)} %bitcast.53), channel_id=1, replica_groups=mesh['groups'=2,'sketch'=4,'context'=2,'example'=2] {'context'}, dimensions={1} | all-to-all | bytes 2097152 | tf_op jit(solution)/shard_map/all_to_all | solution.py:81
  165.3 1.1 copy.19
  166.4 0.0 reduce-scatter.2.cloned.1.call-update
  166.4 0.0 copy-done.3
  166.4 0.0 copy-done.1
  166.4 0.1 fusion.95
  166.5 0.1 reshape.208
  166.6 0.1 mul.118
  166.7 0.1 mul.119
  166.7 0.1 add.191
  166.8 0.1 add.192
  166.9 0.1 mul.115
  167.0 0.0 copy-done
  167.0 14.8 %all_gather.3 = f32[64,2048]{1,0:T(8,128)S(1)} all-gather(f32[16,2048]{1,0:T(8,128)S(1)} %copy-done), channel_id=1, replica_groups=mesh['groups'=2,'sketch'=4,'context'=2,'example'=2] {'sketch'}, dimensions={0}, use_global_device_ids=true | all-gather | bytes 655360 | tf_op jit(solution)/shard_map/all_gather | solution.py:93
  181.7 0.0 reduce-scatter.2.cloned.1.call-done
  181.7 1.4 reshape.205
  183.1 0.3 copy.25
  183.4 0.5 reshape.206
  183.9 0.1 copy.20
  184.0 0.6 fusion.55
  184.6 0.6 convolution_multiply_fusion
  185.2 0.3 copy.24
  185.5 16.6 %gather_fusion = f32[2048]{0:T(1024)S(1)} fusion(f32[32,4096]{1,0:T(8,128)S(1)} %bitcast.49, s32[2048]{0:T(1024)S(1)} %reshape.208), kind=kCustom, calls=%fused_computation | custom fusion | bytes 32768 | tf_op jit(solution)/shard_map/jit(take_along_axis)/gather | solution.py:90
  202.1 0.1 reshape.211
  202.2 0.7 multiply_reduce_fusion
  202.9 0.5 fusion.161
  203.4 6.4 %all-reduce = (f32[1,64]{1,0:T(1,128)S(1)}, f32[1]{0:T(128)}) all-reduce(f32[1,64]{1,0:T(1,128)S(1)} %fusion.161, f32[1]{0:T(128)} %bitcast.14), channel_id=1, replica_groups=mesh['groups'=2,'sketch'=4,'context'=2,'example'=2] {'context','example'}, use_global_device_ids=true, to_apply=%region_1.2 | all-reduce | flops 65 | bytes 520 | tf_op jit(solution)/shard_map/psum | solution.py:97
  210.5 0.5 broadcast_divide_fusion
  (7 shorter events, 0.0 us)
Async XLA Ops:
  61.0 51.9 %all-to-all-start.1 = ((bf16[4,512,512]{2,1,0:T(8,128)(2,1)}), bf16[4,512,512]{2,1,0:T(8,128)(2,1)}, u32[]{:S(2)}, u32[]{:S(2)}) async-start(bf16[4,512,512]{2,1,0:T(8,128)(2,1)} %param.8), calls=%async_computation.1 | async-start | bytes 4194304 | tf_op jit(solution)/shard_map/all_to_all | solution.py:64
  65.5 116.2 %reduce-scatter.2.cloned.1.call-start = ((), (), s32[]{:S(2)}) async-start(), calls=%async_computation.4 | async-start | bytes 1572864 | tf_op jit(solution)/shard_map/reduce_scatter | solution.py:82
  75.0 17.7 %copy-start.2 = (s32[128]{0:T(128)S(1)}, s32[128]{0:T(128)}, u32[]{:S(2)}) copy-start(s32[128]{0:T(128)} %param.10) | copy-start | bytes 1540
  112.9 11.1 %slice-start = ((s8[16777216]{0:T(1024)(128)(4,1)}), s8[4194304]{0:T(1024)(128)(4,1)S(1)}, s32[]{:S(2)}) async-start(s8[16777216]{0:T(1024)(128)(4,1)} %bitcast.50), calls=%async_computation.5 | async-start | bytes 8388608
  112.9 11.1 %slice-start.1 = ((s8[16777216]{0:T(1024)(128)(4,1)}), s8[4194304]{0:T(1024)(128)(4,1)S(1)}, s32[]{:S(2)}) async-start(s8[16777216]{0:T(1024)(128)(4,1)} %bitcast.50), calls=%async_computation.6 | async-start | bytes 8388608
  112.9 11.1 %slice-start.2 = ((s8[16777216]{0:T(1024)(128)(4,1)}), s8[4194304]{0:T(1024)(128)(4,1)S(1)}, s32[]{:S(2)}) async-start(s8[16777216]{0:T(1024)(128)(4,1)} %bitcast.50), calls=%async_computation.7 | async-start | bytes 8388608
  112.9 11.1 %slice-start.3 = ((s8[16777216]{0:T(1024)(128)(4,1)}), s8[4194304]{0:T(1024)(128)(4,1)S(1)}, s32[]{:S(2)}) async-start(s8[16777216]{0:T(1024)(128)(4,1)} %bitcast.50), calls=%async_computation.8 | async-start | bytes 8388608
  124.0 42.4 %copy-start.3 = (s32[32]{0:T(128)S(1)}, s32[32]{0:T(128)}, u32[]{:S(2)}) copy-start(s32[32]{0:T(128)} %param.12) | copy-start | bytes 388
  124.0 42.4 %copy-start.1 = (s32[32]{0:T(128)S(1)}, s32[32]{0:T(128)}, u32[]{:S(2)}) copy-start(s32[32]{0:T(128)} %param.11) | copy-start | bytes 388
  124.0 42.9 %copy-start = (f32[16,2048]{1,0:T(8,128)S(1)}, f32[16,2048]{1,0:T(8,128)}, u32[]{:S(2)}) copy-start(f32[16,2048]{1,0:T(8,128)} %param.13) | copy-start | bytes 393220
Sparse Core Ops, SparseCore 0:
  166.5 5.8 reduce-scatter.1
where the time goes:
time: 219 us; the launch traced here: 218 us
  blocking collectives  91.2 us (42%)
  local copies, waits for them, and re-layouts  47.9 us (22%)
  matrix products  38.5 us (18%)
  waiting for transfers between devices  20.2 us (9%)
  between operations  14.3 us (7%)
  starting transfers between devices  4.51 us (2%)
    all_to_all x1, blocking collectives, body(): lax.all_to_all(activations, 'sketch', split_axis=0, concat_axis=1, tiled=...  54.5 us
    shift_right_arithmetic x5, local copies, waits for them, and re-layouts, sign_table(): bit_values = jnp.bitwise_and(jnp.right_shift(packed[..., None], places), 1)  27.1 us
    dot_general x1, matrix products, body(): partial_value = jnp.dot(signed, col_table, precision=lax.Precision.HIGHEST)  25.7 us
    all_to_all x1, waiting for transfers between devices, body(): lax.all_to_all(out_grads, 'sketch', split_axis=0, concat_axis=1, tiled=True)  20.2 us
    gather x3, local copies, waits for them, and re-layouts, body(): own_sketch = jnp.take_along_axis(column, kept_rows, axis=1).reshape(1, -1)  16.8 us
    all_to_all x1, blocking collectives, body(): lax.all_to_all(split_cols, 'context', split_axis=1, concat_axis=0, tiled=...  15.5 us
    all_gather x1, blocking collectives, body(): lax.all_gather(val_sketch, 'sketch', axis=0, tiled=True)  14.8 us
    dot_general x1, matrix products, body(): jnp.einsum('edt,ekt->dk', arrived_in, arrived_out, preferred_element_type...  11 us
  transfers between devices with their start and end apart: 2, of which 1 were waited for; matrix products, arithmetic and copies ran while one was open for 13% of the time, Pallas kernels for 0%

commit v1 on v0

v1 whole, which is shorter than its diff:
```python
import functools
import math

import jax
import jax.numpy as jnp
from jax import lax
from jax.experimental import pallas as pl
from jax.experimental.pallas import tpu as pltpu
from jax.sharding import PartitionSpec as P

MESH = pl.DeviceIdType.MESH
F32 = jnp.float32
BF16 = jnp.bfloat16
I32 = jnp.int32
LANES = 128
BITS = 16
ROWS = 256
WIDE = 512


def log2(n):
    return n.bit_length() - 1


def sign_of(common):
    for shift in (16, 8, 4, 2, 1):
        common = jnp.bitwise_xor(common, jnp.right_shift(common, shift))
    return (1 - 2 * jnp.bitwise_and(common, 1)).astype(F32)


def iota(shape, axis):
    return lax.broadcasted_iota(I32, shape, axis)


def split(values):
    high = values.astype(BF16)
    return high, (values - high.astype(F32)).astype(BF16)


def place(s, c, k):
    return {"sketch": s, "context": c, "example": k}


def gradient_kernel(sizes, act, grads, words, columns, rows_in, val, part, rows_all, val_all,
                    a_buf, g_buf, gp, gt, table, perm, own_sem,
                    gz_send, gz_recv, az_send, az_recv, vz_send, vz_recv,
                    gx_send, gx_recv, ax_send, ax_recv, r_send, r_recv):
    S, C, E = sizes
    s, c, k = lax.axis_index("sketch"), lax.axis_index("context"), lax.axis_index("example")
    rp, gp_len = act.shape[1], grads.shape[1]
    ah, gh = rp // E, gp_len // C
    total_rows, total_cols = a_buf.shape[0], g_buf.shape[0]
    word_count = words.shape[1]

    barrier = pltpu.get_barrier_semaphore()
    away = [place(lax.rem(s + o, S), c, k) for o in range(1, S)]
    peers = [
        (lax.rem(c + m // E, C), lax.rem(k + m % E, E)) for m in range(1, C * E)
    ]
    for target in away + [place(s, pc, pk) for pc, pk in peers]:
        pl.semaphore_signal(barrier, inc=1, device_id=target, device_id_type=MESH)
    pl.semaphore_wait(barrier, S - 1 + C * E - 1)

    def remote(src, dst, send, recv, target):
        return pltpu.make_async_remote_copy(
            src_ref=src, dst_ref=dst, send_sem=send, recv_sem=recv,
            device_id=target, device_id_type=MESH)

    def g_rows(piece, part_at):
        return pl.ds(pl.multiple_of(piece * gp_len + part_at * gh, gh), gh)

    def a_rows(piece, part_at):
        return pl.ds(pl.multiple_of(piece * rp + part_at * ah, ah), ah)

    def g_send(o):
        t = lax.rem(s + o, S)
        return remote(grads.at[t, pl.ds(pl.multiple_of(c * gh, gh), gh)], g_buf.at[g_rows(s, c)],
                      gz_send.at[o], gz_recv.at[s], place(t, c, k))

    def a_send(o):
        t = lax.rem(s + o, S)
        return remote(act.at[t, pl.ds(pl.multiple_of(k * ah, ah), ah)], a_buf.at[a_rows(s, k)],
                      az_send.at[o], az_recv.at[s], place(t, c, k))

    def v_send(o):
        t = lax.rem(s + o, S)
        return remote(val, val_all.at[s], vz_send.at[o], vz_recv.at[s], place(t, c, k))

    def g_pass(piece, m):
        return remote(g_buf.at[g_rows(piece, c)], g_buf.at[g_rows(piece, c)],
                      gx_send.at[piece, m], gx_recv.at[piece, c], place(s, lax.rem(c + m, C), k))

    def a_pass(piece, m):
        return remote(a_buf.at[a_rows(piece, k)], a_buf.at[a_rows(piece, k)],
                      ax_send.at[piece, m], ax_recv.at[piece, k], place(s, c, lax.rem(k + m, E)))

    def arrived(ref, sem):
        pltpu.make_async_copy(ref, ref, sem).wait()

    me = c * E + k
    started = []

    def start(copy):
        copy.start()
        started.append(copy)

    for o in range(1, S):
        start(g_send(o))
    own_g = pltpu.make_async_copy(
        grads.at[s], g_buf.at[pl.ds(pl.multiple_of(s * gp_len, gp_len), gp_len)], own_sem.at[0])
    own_a = pltpu.make_async_copy(
        act.at[s], a_buf.at[pl.ds(pl.multiple_of(s * rp, rp), rp)], own_sem.at[1])
    own_v = pltpu.make_async_copy(val, val_all.at[s], own_sem.at[2])
    own_g.start()
    own_a.start()
    for m, (pc, pk) in enumerate(peers):
        start(remote(rows_in, rows_all.at[me], r_send.at[m], r_recv.at[me], place(s, pc, pk)))
    rows_all[pl.ds(me, 1)] = rows_in[...][None]

    kept = columns[...]
    for b in range(BITS):
        local = iota((word_count, LANES), 0) * BITS + b
        shift = log2(gp_len)
        full = ((jnp.right_shift(local, shift) * E + k) * gp_len
                + jnp.bitwise_and(local, gp_len - 1))
        table[b * word_count:(b + 1) * word_count, :] = sign_of(
            jnp.bitwise_and(full, kept)).astype(BF16)

    block = perm.shape[0]
    block_words = block // BITS
    blocks = total_cols // block
    row_at, col_at = iota((block, block), 0), iota((block, block), 1)
    source = (jnp.bitwise_and(row_at, block_words - 1) * BITS
              + jnp.right_shift(row_at, log2(block_words)))
    perm[...] = jnp.where(col_at == source, 1.0, 0.0).astype(BF16)

    def permute(at):
        rows = g_buf[pl.ds(pl.multiple_of(at * block, block), block), :]
        moved = jnp.dot(perm[...], rows, preferred_element_type=F32).astype(BF16)
        for b in range(BITS):
            gp[pl.ds(pl.multiple_of(b * word_count + at * block_words, block_words),
                     block_words), :] = moved[b * block_words:(b + 1) * block_words]

    for o in range(1, S):
        piece = lax.rem(s - o + S, S)
        arrived(g_buf.at[g_rows(piece, c)], gz_recv.at[piece])
        start(a_send(o))
        for m in range(1, C):
            start(g_pass(piece, m))
    own_v.start()
    for o in range(1, S):
        start(v_send(o))
    own_g.wait()
    pieces_in_block = max(1, block // gp_len)
    first = s // pieces_in_block
    if blocks * pieces_in_block == S and pieces_in_block == 1:
        permute(s)
    for o in range(1, S):
        piece = lax.rem(s - o + S, S)
        for m in range(1, C):
            other = lax.rem(c + m, C)
            arrived(g_buf.at[g_rows(piece, other)], gx_recv.at[piece, other])
        if blocks * pieces_in_block == S and pieces_in_block == 1:
            permute(piece)
    if not (blocks * pieces_in_block == S and pieces_in_block == 1):
        lax.fori_loop(0, blocks, lambda at, _: (permute(at), 0)[1], 0)
    wide = min(WIDE, total_cols)
    for at in range(total_cols // wide):
        gt[:, at * wide:(at + 1) * wide] = gp[at * wide:(at + 1) * wide, :].T

    row_block = min(ROWS, rp)

    def score_rows(row):
        here = pl.ds(pl.multiple_of(row, row_block), row_block)
        a = a_buf[here, :]
        w = words[here, :]
        total = jnp.zeros((row_block, LANES), F32)
        for at in range(total_cols // wide):
            grad = jnp.dot(a, gt[:, at * wide:(at + 1) * wide], preferred_element_type=F32)
            signed = []
            for bb in range(wide // word_count):
                bit = 1 << (at * (wide // word_count) + bb)
                one = grad[:, bb * word_count:(bb + 1) * word_count]
                signed.append(jnp.where(jnp.bitwise_and(w, bit) != 0, -one, one))
            high, low = split(jnp.concatenate(signed, axis=1))
            side = table[at * wide:(at + 1) * wide, :]
            total = total + jnp.dot(high, side, preferred_element_type=F32)
            total = total + jnp.dot(low, side, preferred_element_type=F32)
        part[here, :] = total

    def score_piece(piece):
        lax.fori_loop(
            0, rp // row_block,
            lambda at, _: (score_rows(piece * rp + at * row_block), 0)[1], 0)

    own_a.wait()
    score_piece(s)
    for o in range(1, S):
        piece = lax.rem(s - o + S, S)
        arrived(a_buf.at[a_rows(piece, k)], az_recv.at[piece])
        for m in range(1, E):
            start(a_pass(piece, m))
        for m in range(1, E):
            other = lax.rem(k + m, E)
            arrived(a_buf.at[a_rows(piece, other)], ax_recv.at[piece, other])
        score_piece(piece)
    for pc, pk in peers:
        arrived(rows_all.at[pc * E + pk], r_recv.at[pc * E + pk])
    own_v.wait()
    for o in range(1, S):
        piece = lax.rem(s - o + S, S)
        arrived(val_all.at[piece], vz_recv.at[piece])
    for copy in started:
        copy.wait_send()


def sketch_kernel(sizes, scale, kr, part, rows_all, out, turned, plain):
    S, C, E = sizes
    c = lax.axis_index("context")
    total_rows = part.shape[0]
    rp = total_rows // S
    in_width = total_rows * C
    q_count = C * E
    block = min(ROWS, total_rows)
    table = sign_of(
        jnp.bitwise_and(iota((block, block), 0), iota((block, block), 1))).astype(BF16)
    mixed = []
    for at in range(total_rows // block):
        both = jnp.concatenate(split(part[at * block:(at + 1) * block, :]), axis=1)
        got = jnp.dot(table, both, preferred_element_type=F32)
        mixed.append(got[:, :LANES] + got[:, LANES:])
    step = 1
    while step < len(mixed):
        nxt = list(mixed)
        for at in range(len(mixed)):
            if at & step == 0:
                nxt[at] = mixed[at] + mixed[at + step]
                nxt[at + step] = mixed[at] - mixed[at + step]
        mixed = nxt
        step *= 2
    for at, values in enumerate(mixed):
        for b in range(0, block, LANES):
            turned[at * block + b:at * block + b + LANES, :] = values[b:b + LANES, :].T

    lane = iota((1, LANES), 1)
    per = LANES // q_count
    begin = jnp.zeros((1, LANES), I32)
    half = jnp.zeros((1, LANES), I32)
    for q in range(q_count):
        mine = jnp.right_shift(lane, log2(per)) == q
        begin = jnp.where(mine, rows_all[q, 0:1, :], begin)
        half = jnp.where(mine, rows_all[q, 1:2, :], half)
    fold = LANES // kr
    high_rows = LANES // fold
    shape = (high_rows, LANES)
    wide_lane = iota(shape, 1)
    at_i = jnp.bitwise_and(wide_lane, kr - 1)
    group = jnp.right_shift(wide_lane, log2(kr))

    def down(vector):
        plain[...] = jnp.broadcast_to(vector, (LANES, LANES)).T
        got = plain[pl.ds(0, high_rows, stride=fold), :]
        for f in range(1, fold):
            got = jnp.where(group == f, plain[pl.ds(f, high_rows, stride=fold), :], got)
        return got

    row = jnp.bitwise_and(down(begin) + at_i * (2 * down(half) + 1), in_width - 1)
    piece_bits, context_bits = log2(rp), log2(C)
    sign = sign_of(jnp.bitwise_and(jnp.bitwise_and(jnp.right_shift(row, piece_bits), C - 1), c))
    local = (jnp.left_shift(jnp.right_shift(row, piece_bits + context_bits), piece_bits)
             + jnp.bitwise_and(row, rp - 1))
    in_block = jnp.bitwise_and(local, LANES - 1)
    which = jnp.right_shift(local, log2(LANES))
    picked = jnp.zeros(shape, F32)
    for at in range(total_rows // LANES):
        found = None
        for f in range(fold):
            values = turned[pl.ds(at * LANES + f, high_rows, stride=fold), :]
            got = jnp.take_along_axis(values, in_block, axis=1, mode="promise_in_bounds")
            found = got if found is None else jnp.where(group == f, got, found)
        picked = jnp.where(which == at, found, picked)
    out[...] = picked * sign * scale


def score_kernel(sizes, sketch, val, out, parts, sums, send, recv, send2, recv2):
    S, C, E = sizes
    s, c, k = lax.axis_index("sketch"), lax.axis_index("context"), lax.axis_index("example")
    q_count = C * E
    per = sketch.shape[0] // q_count
    nv = val.shape[0]
    me = c * E + k
    barrier = pltpu.get_barrier_semaphore()
    peers = [
        (lax.rem(c + m // E, C), lax.rem(k + m % E, E)) for m in range(1, q_count)
    ]
    for pc, pk in peers:
        pl.semaphore_signal(barrier, inc=1, device_id=place(s, pc, pk), device_id_type=MESH)
    pl.semaphore_wait(barrier, q_count - 1)

    copies = []
    for m, (pc, pk) in enumerate(peers):
        rows = pl.ds(pl.multiple_of((pc * E + pk) * per, per), per)
        copies.append(pltpu.make_async_remote_copy(
            src_ref=sketch.at[rows], dst_ref=parts.at[me], send_sem=send.at[m],
            recv_sem=recv.at[me], device_id=place(s, pc, pk), device_id_type=MESH))
        copies[-1].start()
    parts[pl.ds(me, 1)] = sketch[pl.ds(pl.multiple_of(me * per, per), per), :][None]
    for pc, pk in peers:
        ref = parts.at[pc * E + pk]
        pltpu.make_async_copy(ref, ref, recv.at[pc * E + pk]).wait()
    own = parts[0]
    for q in range(1, q_count):
        own = own + parts[q]
    total = jnp.zeros((nv, LANES), F32)
    for r in range(per):
        total = total + val[:, r * LANES:(r + 1) * LANES] * own[r:r + 1, :]
    squares = jnp.sum(own * own, axis=0, keepdims=True)
    tall = jnp.concatenate(
        [total, squares, jnp.zeros((LANES - nv - 1, LANES), F32)], axis=0)
    mine = jnp.sum(tall.T, axis=0, keepdims=True)
    sums[pl.ds(me, 1)] = jnp.broadcast_to(mine, (8, LANES))[None]
    for m, (pc, pk) in enumerate(peers):
        copies.append(pltpu.make_async_remote_copy(
            src_ref=sums.at[me], dst_ref=sums.at[me], send_sem=send2.at[m],
            recv_sem=recv2.at[me], device_id=place(s, pc, pk), device_id_type=MESH))
        copies[-1].start()
    for pc, pk in peers:
        ref = sums.at[pc * E + pk]
        pltpu.make_async_copy(ref, ref, recv2.at[pc * E + pk]).wait()
    all_sums = sums[0]
    for q in range(1, q_count):
        all_sums = all_sums + sums[q]
    out[...] = all_sums[0:1, :nv] / jnp.sqrt(all_sums[0:1, nv:nv + 1] + 1e-06)
    for copy in copies:
        copy.wait_send()


def body(activations, out_grads, sign_bits, keep_cols, row_start, row_step, val_sketch):
    S, C, E = lax.axis_size("sketch"), lax.axis_size("context"), lax.axis_size("example")
    sizes = (S, C, E)
    rp, tokens = activations.shape[1:]
    gp_len = out_grads.shape[1]
    local_rows, local_cols = S * rp, S * gp_len
    in_width, out_width = local_rows * C, local_cols * E
    kept = keep_cols.shape[0]
    q_count = C * E
    keep = val_sketch.shape[1] * q_count
    kr = keep // kept
    nv = val_sketch.shape[0] * S
    words = sign_bits.reshape(local_rows, -1)
    columns = (jnp.arange(kept, dtype=I32) * (out_width // kept) + keep_cols)[None, :]
    rows_in = jnp.concatenate(
        [jnp.tile(row_start, q_count)[None], jnp.tile(row_step, q_count)[None],
         jnp.zeros((6, kept), I32)], axis=0)
    vmem = pl.BlockSpec(memory_space=pltpu.VMEM)
    hbm = pl.BlockSpec(memory_space=pl.ANY)
    dma = pltpu.SemaphoreType.DMA
    block = min(WIDE, local_cols)
    part, rows_all, val_all = pl.pallas_call(
        functools.partial(gradient_kernel, sizes),
        out_shape=(
            jax.ShapeDtypeStruct((local_rows, kept), F32),
            jax.ShapeDtypeStruct((q_count, 8, kept), I32),
            jax.ShapeDtypeStruct((S,) + val_sketch.shape, F32),
        ),
        in_specs=[hbm, hbm, vmem, vmem, vmem, hbm],
        out_specs=(vmem, vmem, hbm),
        scratch_shapes=[
            pltpu.VMEM((local_rows, tokens), BF16),
            pltpu.VMEM((local_cols, tokens), BF16),
            pltpu.VMEM((local_cols, tokens), BF16),
            pltpu.VMEM((tokens, local_cols), BF16),
            pltpu.VMEM((local_cols, kept), BF16),
            pltpu.VMEM((block, block), BF16),
            dma((3,)),
            dma((S,)), dma((S,)), dma((S,)), dma((S,)), dma((S,)), dma((S,)),
            dma((S, C)), dma((S, C)), dma((S, E)), dma((S, E)),
            dma((q_count,)), dma((q_count,)),
        ],
        compiler_params=pltpu.CompilerParams(
            collective_id=0, has_side_effects=True, vmem_limit_bytes=44 * 2**20),
        cost_estimate=pl.CostEstimate(
            flops=2 * local_rows * local_cols * (tokens + 2 * kept),
            bytes_accessed=2 * (local_rows + local_cols) * tokens, transcendentals=0),
        name="gradient",
    )(activations, out_grads, words, columns, rows_in, val_sketch)
    sketch = pl.pallas_call(
        functools.partial(
            sketch_kernel, sizes, 1.0 / (math.sqrt(in_width) * math.sqrt(out_width)), kr),
        out_shape=jax.ShapeDtypeStruct((keep // LANES, LANES), F32),
        in_specs=[vmem, vmem],
        out_specs=vmem,
        scratch_shapes=[
            pltpu.VMEM((local_rows, LANES), F32),
            pltpu.VMEM((LANES, LANES), I32),
        ],
        compiler_params=pltpu.CompilerParams(vmem_limit_bytes=32 * 2**20),
        name="sketch",
    )(part, rows_all)
    return pl.pallas_call(
        functools.partial(score_kernel, sizes),
        out_shape=jax.ShapeDtypeStruct((1, nv), F32),
        in_specs=[vmem, vmem],
        out_specs=vmem,
        scratch_shapes=[
            pltpu.VMEM((q_count, keep // LANES // q_count, LANES), F32),
            pltpu.VMEM((q_count, 8, LANES), F32),
            dma((q_count,)), dma((q_count,)), dma((q_count,)), dma((q_count,)),
        ],
        compiler_params=pltpu.CompilerParams(
            collective_id=1, has_side_effects=True, vmem_limit_bytes=32 * 2**20),
        name="score",
    )(sketch, val_all.reshape(nv, -1))


def solution(mesh):
    placed = (
        P("groups", ("sketch", "context"), None),
        P("groups", ("sketch", "example"), None),
        P(None, "context", None, "example", None),
        P(),
        P(("context", "example")),
        P(("context", "example")),
        P("sketch", ("context", "example")),
    )
    return jax.shard_map(
        body, mesh=mesh, in_specs=placed, out_specs=P(("groups", "sketch"), None), check_vma=False
    )
```

time: 219 us -> 82.3 us (0.38)
  the two profiles are of different devices: /device:TPU:0 before, /device:TPU:25 now
where the time goes in v1:
time: 82.3 us; the launch traced here: 82 us
  Pallas kernels  73.9 us (90%)
  local copies, waits for them, and re-layouts  7.38 us (9%)
    pallas_call x1, Pallas kernels, body(): pl.pallas_call(functools.partial(gradient_kernel, sizes), out_shape=(jax....  65.3 us
    pallas_call x1, Pallas kernels, body(): pl.pallas_call(functools.partial(score_kernel, sizes), out_shape=jax.Shap...  7.15 us
    unnamed x9, local copies, waits for them, and re-layouts  5.82 us

profile of v1, /device:TPU:25, one launch (start us, length us, event | category | flops | bytes accessed | tf_op | source)
XLA Modules:
  0.0 82.0 jit_solution(14442401725972373146)
XLA Ops:
  0.0 0.7 add_bitcast_fusion.columns
  0.7 0.1 pad.2.clone
  0.7 0.7 tile.4
  1.4 0.1 broadcast_in_dim_tile.6
  1.5 0.7 tile.5
  2.1 0.1 broadcast_in_dim_tile.7
  2.2 0.1 add_add_fusion.rows_in
  2.3 0.0 copy-start
  2.3 1.6 %copy-done = bf16[4,512,512]{2,1,0:T(8,128)(2,1)S(1)} copy-done((bf16[4,512,512]{2,1,0:T(8,128)(2,1)S(1)}, bf16[4,512,512]{2,1,0:T(8,128)(2,1)}, u32[]{:S(2)}) %copy-start) | copy-done | bytes 2097176
  3.9 0.0 copy-start.1
  3.9 1.6 %copy-done.1 = bf16[4,512,512]{2,1,0:T(8,128)(2,1)S(1)} copy-done((bf16[4,512,512]{2,1,0:T(8,128)(2,1)S(1)}, bf16[4,512,512]{2,1,0:T(8,128)(2,1)}, u32[]{:S(2)}) %copy-start.1) | copy-done | bytes 2097176
  5.5 0.0 copy-start.2
  5.5 1.2 %copy-done.2 = s32[4,1,512,1,128]{4,3,2,1,0:T(1,128)S(1)} copy-done((s32[4,1,512,1,128]{4,3,2,1,0:T(1,128)S(1)}, s32[4,1,512,1,128]{4,3,2,1,0:T(1,128)}, u32[]{:S(2)}) %copy-start.2) | copy-done | bytes 1048600
  6.7 0.0 copy-start.3
  6.7 0.9 %copy-done.3 = f32[16,2048]{1,0:T(8,128)S(1)} copy-done((f32[16,2048]{1,0:T(8,128)S(1)}, f32[16,2048]{1,0:T(8,128)}, u32[]{:S(2)}) %copy-start.3) | copy-done | bytes 131096
  7.6 65.3 %gradient.1 = (f32[2048,128]{1,0:T(8,128)S(1)}, s32[4,8,128]{2,1,0:T(8,128)S(1)}, f32[4,16,2048]{2,1,0:T(8,128)S(1)}) custom-call(bf16[4,512,512]{2,1,0:T(8,128)(2,1)S(1)} %copy-done, bf16[4,512,512]{2,1,0:T(8,128)(2,1)S(1)} %copy-done.1, s32[2048,128]{1,0:T(8,128)S(1)} %bitcast.5, s32[1,128]{1,0:T(1,128)S(1)} %add_bitcast_fusion.columns, ...), custom_call_target="tpu_custom_call" | custom-call | flops 6442450944 | bytes 4194304 | tf_op jit(solution)/shard_map/gradient/pallas_call | solution.py:359
  72.9 1.5 %sketch.1 = f32[64,128]{1,0:T(8,128)S(1)} custom-call(f32[2048,128]{1,0:T(8,128)S(1)} %get-tuple-element.8.part, s32[4,8,128]{2,1,0:T(8,128)S(1)} %get-tuple-element.9.rows_all), custom_call_target="tpu_custom_call" | custom-call | tf_op jit(solution)/shard_map/sketch/pallas_call | solution.py:387
  74.3 7.1 %score.1 = f32[1,64]{1,0:T(1,128)S(1)} custom-call(f32[64,128]{1,0:T(8,128)S(1)} %sketch.1, f32[64,2048]{1,0:T(8,128)S(1)} %bitcast.4), custom_call_target="tpu_custom_call" | custom-call | tf_op jit(solution)/shard_map/score/pallas_call | solution.py:400
  81.5 0.5 copy.9
  (1 shorter events, 0.0 us)
Async XLA Ops:
  2.3 1.6 %copy-start = (bf16[4,512,512]{2,1,0:T(8,128)(2,1)S(1)}, bf16[4,512,512]{2,1,0:T(8,128)(2,1)}, u32[]{:S(2)}) copy-start(bf16[4,512,512]{2,1,0:T(8,128)(2,1)} %act.1) | copy-start | bytes 6291460
  3.9 1.6 %copy-start.1 = (bf16[4,512,512]{2,1,0:T(8,128)(2,1)S(1)}, bf16[4,512,512]{2,1,0:T(8,128)(2,1)}, u32[]{:S(2)}) copy-start(bf16[4,512,512]{2,1,0:T(8,128)(2,1)} %grads.1) | copy-start | bytes 6291460
  5.5 1.2 %copy-start.2 = (s32[4,1,512,1,128]{4,3,2,1,0:T(1,128)S(1)}, s32[4,1,512,1,128]{4,3,2,1,0:T(1,128)}, u32[]{:S(2)}) copy-start(s32[4,1,512,1,128]{4,3,2,1,0:T(1,128)} %param.9) | copy-start | bytes 3145732
  6.7 0.9 %copy-start.3 = (f32[16,2048]{1,0:T(8,128)S(1)}, f32[16,2048]{1,0:T(8,128)}, u32[]{:S(2)}) copy-start(f32[16,2048]{1,0:T(8,128)} %val.1) | copy-start | bytes 393220

commit v2 on v1

v2 whole, which is shorter than its diff:
```python
import functools
import math

import jax
import jax.numpy as jnp
from jax import lax
from jax.experimental import pallas as pl
from jax.experimental.pallas import tpu as pltpu
from jax.sharding import PartitionSpec as P

MESH = pl.DeviceIdType.MESH
F32 = jnp.float32
BF16 = jnp.bfloat16
I32 = jnp.int32
LANES = 128
BITS = 16
ROWS = 256
WIDE = 512


def log2(n):
    return n.bit_length() - 1


def sign_of(common):
    for shift in (16, 8, 4, 2, 1):
        common = jnp.bitwise_xor(common, jnp.right_shift(common, shift))
    return (1 - 2 * jnp.bitwise_and(common, 1)).astype(F32)


def iota(shape, axis):
    return lax.broadcasted_iota(I32, shape, axis)


def split(values):
    high = values.astype(BF16)
    return high, (values - high.astype(F32)).astype(BF16)


def place(s, c, k):
    return {"sketch": s, "context": c, "example": k}


def each(count, step):
    if count <= 32:
        for at in range(1, count):
            step(at)
    else:
        lax.fori_loop(1, count, lambda at, _: (step(at), 0)[1], 0)


def kernel(sizes, scale, kr, act, grads, words_in, columns_in, begin_in, half_in, val_in, out,
           a_buf, g_buf, gp, gt, table, perm, hada, words, columns, begins, halves, val,
           part, turned, plain, ring, sketch, parts, sums,
           own_sem, gz_send, gz_recv, az_send, az_recv, gx_send, gx_recv, ax_send, ax_recv,
           r_send, r_recv, p_send, p_recv, s_send, s_recv):
    S, C, E = sizes
    Q = C * E
    s, c, k = lax.axis_index("sketch"), lax.axis_index("context"), lax.axis_index("example")
    me = c * E + k
    rp, gp_len = act.shape[1], grads.shape[1]
    gh = gp_len // C
    row_block = min(ROWS, rp)
    halves_of = rp // row_block
    ah = row_block // E
    total_rows, total_cols = a_buf.shape[0], g_buf.shape[0]
    in_width, out_width = total_rows * C, total_cols * E
    word_count = words.shape[1]
    kept = columns.shape[1]

    def member(m):
        t = lax.rem(s + lax.div(m, Q), S)
        q = lax.rem(me + lax.rem(m, Q), Q)
        return t, q

    def spot(t, q):
        return place(t, lax.div(q, E), lax.rem(q, E))

    barrier = pltpu.get_barrier_semaphore()

    def greet(m):
        pl.semaphore_signal(barrier, inc=1, device_id=spot(*member(jnp.int32(m))),
                            device_id_type=MESH)

    local = [
        pltpu.make_async_copy(src, dst, own_sem.at[at]) for at, (src, dst) in enumerate((
            (begin_in, begins), (half_in, halves), (columns_in, columns),
            (grads.at[s], g_buf.at[pl.ds(pl.multiple_of(s * gp_len, gp_len), gp_len)]),
            (act.at[s], a_buf.at[pl.ds(pl.multiple_of(s * rp, rp), rp)]),
            (words_in, words), (val_in, val)))
    ]
    each(S * Q, greet)
    for copy in local[:3]:
        copy.start()
    pl.semaphore_wait(barrier, S * Q - 1)

    def remote(src, dst, send, recv, target):
        return pltpu.make_async_remote_copy(
            src_ref=src, dst_ref=dst, send_sem=send, recv_sem=recv,
            device_id=target, device_id_type=MESH)

    def g_rows(piece, part_at):
        return pl.ds(pl.multiple_of(piece * gp_len + part_at * gh, gh), gh)

    def a_rows(piece, h, part_at):
        return pl.ds(pl.multiple_of(piece * rp + h * row_block + part_at * ah, ah), ah)

    def g_send(o):
        t = lax.rem(s + o, S)
        return remote(grads.at[t, pl.ds(pl.multiple_of(c * gh, gh), gh)], g_buf.at[g_rows(s, c)],
                      gz_send.at[o], gz_recv.at[s], place(t, c, k))

    def a_send(o, h):
        t = lax.rem(s + o, S)
        return remote(act.at[t, pl.ds(pl.multiple_of(h * row_block + k * ah, ah), ah)],
                      a_buf.at[a_rows(s, h, k)], az_send.at[o, h], az_recv.at[s, h],
                      place(t, c, k))

    def g_pass(piece, m):
        return remote(g_buf.at[g_rows(piece, c)], g_buf.at[g_rows(piece, c)],
                      gx_send.at[piece, m], gx_recv.at[piece, c], place(s, lax.rem(c + m, C), k))

    def a_pass(piece, h, m):
        rows = a_rows(piece, h, k)
        return remote(a_buf.at[rows], a_buf.at[rows], ax_send.at[piece, h, m],
                      ax_recv.at[piece, h, k], place(s, c, lax.rem(k + m, E)))

    def arrived(ref, sem):
        pltpu.make_async_copy(ref, ref, sem).wait()

    started = []

    def start(copy):
        copy.start()
        started.append(copy)

    for o in range(1, S):
        start(g_send(o))
    for copy in local[3:]:
        copy.start()

    for copy in local[:2]:
        copy.wait()
    per_q = kept // Q
    ring[pl.ds(me, 1)] = jnp.zeros((1, 8, kept), I32)
    for q in range(Q):
        ring[me, 0:1, q * per_q:(q + 1) * per_q] = begins[...]
        ring[me, 1:2, q * per_q:(q + 1) * per_q] = halves[...]
    for m in range(1, Q):
        q = lax.rem(me + m, Q)
        start(remote(ring.at[me], ring.at[me], r_send.at[m], r_recv.at[me], spot(s, q)))

    local[2].wait()
    width = out_width // kept
    kept_cols = columns[...] + iota((1, kept), 1) * width
    for b in range(BITS):
        at = iota((word_count, kept), 0) * BITS + b
        full = ((jnp.right_shift(at, log2(gp_len)) * E + k) * gp_len
                + jnp.bitwise_and(at, gp_len - 1))
        table[b * word_count:(b + 1) * word_count, :] = sign_of(
            jnp.bitwise_and(full, kept_cols)).astype(BF16)
    hada[...] = sign_of(jnp.bitwise_and(
        iota((row_block, row_block), 0), iota((row_block, row_block), 1))).astype(BF16)

    block = perm.shape[0]
    block_words = block // BITS
    blocks = total_cols // block
    row_at, col_at = iota((block, block), 0), iota((block, block), 1)
    source = (jnp.bitwise_and(row_at, block_words - 1) * BITS
              + jnp.right_shift(row_at, log2(block_words)))
    perm[...] = jnp.where(col_at == source, 1.0, 0.0).astype(BF16)

    def permute(at):
        rows = g_buf[pl.ds(pl.multiple_of(at * block, block), block), :]
        moved = jnp.dot(perm[...], rows, preferred_element_type=F32).astype(BF16)
        for b in range(BITS):
            gp[pl.ds(pl.multiple_of(b * word_count + at * block_words, block_words),
                     block_words), :] = moved[b * block_words:(b + 1) * block_words]

    for o in range(1, S):
        piece = lax.rem(s - o + S, S)
        arrived(g_buf.at[g_rows(piece, c)], gz_recv.at[piece])
        for h in range(halves_of):
            start(a_send(o, h))
        for m in range(1, C):
            start(g_pass(piece, m))
    local[3].wait()
    piece_blocks = block == gp_len
    if piece_blocks:
        permute(s)
    for o in range(1, S):
        piece = lax.rem(s - o + S, S)
        for m in range(1, C):
            other = lax.rem(c + m, C)
            arrived(g_buf.at[g_rows(piece, other)], gx_recv.at[piece, other])
        if piece_blocks:
            permute(piece)
    if not piece_blocks:
        lax.fori_loop(0, blocks, lambda at, _: (permute(at), 0)[1], 0)
    wide = min(WIDE, total_cols)
    for at in range(total_cols // wide):
        gt[:, at * wide:(at + 1) * wide] = gp[at * wide:(at + 1) * wide, :].T

    def score_rows(row):
        here = pl.ds(pl.multiple_of(row, row_block), row_block)
        a = a_buf[here, :]
        w = words[here, :]
        total = jnp.zeros((row_block, kept), F32)
        for at in range(total_cols // wide):
            grad = jnp.dot(a, gt[:, at * wide:(at + 1) * wide], preferred_element_type=F32)
            signed = []
            for bb in range(wide // word_count):
                bit = 1 << (at * (wide // word_count) + bb)
                one = grad[:, bb * word_count:(bb + 1) * word_count]
                signed.append(jnp.where(jnp.bitwise_and(w, bit) != 0, -one, one))
            high, low = split(jnp.concatenate(signed, axis=1))
            side = table[at * wide:(at + 1) * wide, :]
            total = total + jnp.dot(high, side, preferred_element_type=F32)
            total = total + jnp.dot(low, side, preferred_element_type=F32)
        got = jnp.dot(hada[...], jnp.concatenate(split(total), axis=1),
                      preferred_element_type=F32)
        part[here, :] = got[:, :kept] + got[:, kept:]

    local[4].wait()
    local[5].wait()
    lax.fori_loop(0, halves_of, lambda h, _: (score_rows(s * rp + h * row_block), 0)[1], 0)
    for o in range(1, S):
        piece = lax.rem(s - o + S, S)
        for h in range(halves_of):
            arrived(a_buf.at[a_rows(piece, h, k)], az_recv.at[piece, h])
            for m in range(1, E):
                start(a_pass(piece, h, m))
            for m in range(1, E):
                other = lax.rem(k + m, E)
                arrived(a_buf.at[a_rows(piece, h, other)], ax_recv.at[piece, h, other])
            score_rows(piece * rp + h * row_block)

    mixed = [part[at:at + row_block, :] for at in range(0, total_rows, row_block)]
    step = 1
    while step < len(mixed):
        nxt = list(mixed)
        for at in range(len(mixed)):
            if at & step == 0:
                nxt[at] = mixed[at] + mixed[at + step]
                nxt[at + step] = mixed[at] - mixed[at + step]
        mixed = nxt
        step *= 2
    whole = mixed if row_block >= LANES else [
        jnp.concatenate(mixed[at:at + LANES // row_block], axis=0)
        for at in range(0, len(mixed), LANES // row_block)]
    turned_rows = 0
    for values in whole:
        for b in range(0, values.shape[0], LANES):
            turned[turned_rows:turned_rows + LANES, :] = values[b:b + LANES, :].T
            turned_rows += LANES

    for m in range(1, Q):
        q = lax.rem(me + m, Q)
        arrived(ring.at[q], r_recv.at[q])
    lane = iota((1, kept), 1)
    begin = jnp.zeros((1, kept), I32)
    half = jnp.zeros((1, kept), I32)
    for q in range(Q):
        mine = jnp.right_shift(lane, log2(per_q)) == q
        begin = jnp.where(mine, ring[q, 0:1, :], begin)
        half = jnp.where(mine, ring[q, 1:2, :], half)
    fold = LANES // kr
    high_rows = kept // fold
    shape = (high_rows, LANES)
    wide_lane = iota(shape, 1)
    at_i = jnp.bitwise_and(wide_lane, kr - 1)
    group = jnp.right_shift(wide_lane, log2(kr))

    def down(vector):
        plain[...] = jnp.broadcast_to(vector, (kept, kept)).T
        got = plain[pl.ds(0, high_rows, stride=fold), :]
        for f in range(1, fold):
            got = jnp.where(group == f, plain[pl.ds(f, high_rows, stride=fold), :], got)
        return got

    row = jnp.bitwise_and(down(begin) + at_i * (2 * down(half) + 1), in_width - 1)
    piece_bits, context_bits = log2(rp), log2(C)
    sign = sign_of(jnp.bitwise_and(jnp.bitwise_and(jnp.right_shift(row, piece_bits), C - 1), c))
    held = (jnp.left_shift(jnp.right_shift(row, piece_bits + context_bits), piece_bits)
            + jnp.bitwise_and(row, rp - 1))
    in_block = jnp.bitwise_and(held, LANES - 1)
    which = jnp.right_shift(held, log2(LANES))
    picked = jnp.zeros(shape, F32)
    for at in range(total_rows // LANES):
        found = None
        for f in range(fold):
            values = turned[pl.ds(at * LANES + f, high_rows, stride=fold), :]
            got = jnp.take_along_axis(values, in_block, axis=1, mode="promise_in_bounds")
            found = got if found is None else jnp.where(group == f, got, found)
        picked = jnp.where(which == at, found, picked)
    sketch[...] = picked * sign * scale

    per = high_rows // Q
    mine_at = s * Q + me

    def q_rows(q):
        return pl.ds(pl.multiple_of(q * per, per), per)

    def p_copy(m):
        t, q = member(jnp.int32(m))
        return remote(sketch.at[q_rows(q)], parts.at[mine_at], p_send.at[m], p_recv.at[mine_at],
                      spot(t, q))

    each(S * Q, lambda m: p_copy(m).start())
    parts[pl.ds(mine_at, 1)] = sketch[q_rows(me), :][None]
    local[6].wait()

    def p_arrived(m):
        t, q = member(jnp.int32(m))
        arrived(parts.at[t * Q + q], p_recv.at[t * Q + q])

    each(S * Q, p_arrived)
    nvl = val.shape[0]
    nv = nvl * S
    out_lane = iota((1, LANES), 1)

    def products(e):
        own = parts[e * Q]
        for q in range(1, Q):
            own = own + parts[e * Q + q]
        total = jnp.zeros((nvl, LANES), F32)
        for r in range(per):
            total = total + val[:, r * LANES:(r + 1) * LANES] * own[r:r + 1, :]
        squares = jnp.sum(own * own, axis=0, keepdims=True)
        tall = jnp.concatenate(
            [total, squares, jnp.zeros((LANES - nvl - 1, LANES), F32)], axis=0)
        line = jnp.sum(tall.T, axis=0, keepdims=True)
        norm = jnp.sum(squares, axis=1, keepdims=True)
        mine = pltpu.roll(jnp.where(out_lane < nvl, line, 0.0), s * nvl, axis=1)
        mine = jnp.where(out_lane == nv, norm * (s == 0).astype(F32), mine)
        return jnp.broadcast_to(mine, (8, LANES))

    answers = part

    def e_rows(e):
        return pl.ds(pl.multiple_of(e * 8, 8), 8)

    if S <= 16:
        for e in range(S):
            answers[e * 8:(e + 1) * 8, :] = products(e)
    else:
        def put(e, carry):
            answers[e_rows(e), :] = products(e)
            return carry
        lax.fori_loop(0, S, put, 0)

    def s_copy(m):
        t, q = member(jnp.int32(m))
        return remote(answers.at[e_rows(t)], sums.at[mine_at], s_send.at[m], s_recv.at[mine_at],
                      spot(t, q))

    each(S * Q, lambda m: s_copy(m).start())
    sums[pl.ds(mine_at, 1)] = answers[e_rows(s), :][None]

    def s_arrived(m):
        t, q = member(jnp.int32(m))
        arrived(sums.at[t * Q + q], s_recv.at[t * Q + q])

    each(S * Q, s_arrived)
    all_sums = sums[0]
    for at in range(1, S * Q):
        all_sums = all_sums + sums[at]
    out[...] = all_sums[0:1, :nv] / jnp.sqrt(all_sums[0:1, nv:nv + 1] + 1e-06)
    for copy in started:
        copy.wait_send()
    each(S * Q, lambda m: p_copy(m).wait_send())
    each(S * Q, lambda m: s_copy(m).wait_send())


def body(activations, out_grads, sign_bits, keep_cols, row_start, row_step, val_sketch):
    S, C, E = lax.axis_size("sketch"), lax.axis_size("context"), lax.axis_size("example")
    Q = C * E
    rp, tokens = activations.shape[1:]
    gp_len = out_grads.shape[1]
    local_rows, local_cols = S * rp, S * gp_len
    in_width, out_width = local_rows * C, local_cols * E
    kept = keep_cols.shape[0]
    keep = val_sketch.shape[1] * Q
    kr = keep // kept
    nv = val_sketch.shape[0] * S
    words = sign_bits.reshape(local_rows, -1)
    row_block = min(ROWS, rp)
    halves = rp // row_block
    hbm = pl.BlockSpec(memory_space=pl.ANY)
    dma = pltpu.SemaphoreType.DMA
    block = min(WIDE, local_cols)
    return pl.pallas_call(
        functools.partial(
            kernel, (S, C, E), 1.0 / (math.sqrt(in_width) * math.sqrt(out_width)), kr),
        out_shape=jax.ShapeDtypeStruct((1, nv), F32),
        in_specs=[hbm] * 7,
        out_specs=pl.BlockSpec(memory_space=pltpu.VMEM),
        scratch_shapes=[
            pltpu.VMEM((local_rows, tokens), BF16),
            pltpu.VMEM((local_cols, tokens), BF16),
            pltpu.VMEM((local_cols, tokens), BF16),
            pltpu.VMEM((tokens, local_cols), BF16),
            pltpu.VMEM((local_cols, kept), BF16),
            pltpu.VMEM((block, block), BF16),
            pltpu.VMEM((row_block, row_block), BF16),
            pltpu.VMEM(words.shape, I32),
            pltpu.VMEM((1, kept), I32),
            pltpu.VMEM((1, kept // Q), I32),
            pltpu.VMEM((1, kept // Q), I32),
            pltpu.VMEM(val_sketch.shape, F32),
            pltpu.VMEM((local_rows, kept), F32),
            pltpu.VMEM((local_rows, LANES), F32),
            pltpu.VMEM((kept, kept), I32),
            pltpu.VMEM((Q, 8, kept), I32),
            pltpu.VMEM((keep // LANES, LANES), F32),
            pltpu.VMEM((S * Q, keep // LANES // Q, LANES), F32),
            pltpu.VMEM((S * Q, 8, LANES), F32),
            dma((7,)),
            dma((S,)), dma((S,)), dma((S, halves)), dma((S, halves)),
            dma((S, C)), dma((S, C)), dma((S, halves, E)), dma((S, halves, E)),
            dma((Q,)), dma((Q,)),
            dma((S * Q,)), dma((S * Q,)), dma((S * Q,)), dma((S * Q,)),
        ],
        compiler_params=pltpu.CompilerParams(
            collective_id=0, has_side_effects=True, vmem_limit_bytes=60 * 2**20),
        cost_estimate=pl.CostEstimate(
            flops=2 * local_rows * local_cols * (tokens + 2 * kept),
            bytes_accessed=2 * (local_rows + local_cols) * tokens, transcendentals=0),
        name="scores",
    )(activations, out_grads, words, keep_cols[None], row_start[None], row_step[None], val_sketch)


def solution(mesh):
    placed = (
        P("groups", ("sketch", "context"), None),
        P("groups", ("sketch", "example"), None),
        P(None, "context", None, "example", None),
        P(),
        P(("context", "example")),
        P(("context", "example")),
        P("sketch", ("context", "example")),
    )
    return jax.shard_map(
        body, mesh=mesh, in_specs=placed, out_specs=P(("groups", "sketch"), None), check_vma=False
    )
```

time: 82.3 us -> 83.7 us (1.017)
  the two profiles are of different devices: /device:TPU:25 before, /device:TPU:0 now
where the time goes in v2:
time: 83.7 us; the launch traced here: 83.6 us
  Pallas kernels  82.4 us (98%)
  local copies, waits for them, and re-layouts  1.19 us (1%)
    pallas_call x1, Pallas kernels, body(): pl.pallas_call(functools.partial(kernel, (S, C, E), 1.0 / (math.sqrt(in_w...  82.4 us

profile of v2, /device:TPU:0, one launch (start us, length us, event | category | flops | bytes accessed | tf_op | source)
XLA Modules:
  0.0 83.6 jit_solution(2823066581397613510)
XLA Ops:
  0.0 82.4 %scores.1 = f32[1,64]{1,0:T(1,128)} custom-call(bf16[4,512,512]{2,1,0:T(8,128)(2,1)} %act.1, bf16[4,512,512]{2,1,0:T(8,128)(2,1)} %grads.1, s32[2048,128]{1,0:T(8,128)} %bitcast.4, s32[1,128]{1,0:T(1,128)} %bitcast.5, s32[1,32]{1,0:T(1,128)} %bitcast.6, s32[1,32]{1,0:T(1,128)} %bitcast.7, f32[16,2048]{1,0:T(8,128)} %val_in.1), custom_call_target="tpu_custom_call" | custom-call | flops 6442450944 | bytes 4194304 | tf_op jit(solution)/shard_map/scores/pallas_call | solution.py:392
  82.4 1.2 %copy.9 = f32[1,64]{1,0:T(1,128)} copy(f32[1,64]{1,0:T(1,128)} %scores.1) | data formatting | bytes 512

commit v3 on v2

--- a/solution.py
+++ b/solution.py
@@ -42,11 +42,7 @@
 
 
 def each(count, step):
-    if count <= 32:
-        for at in range(1, count):
-            step(at)
-    else:
-        lax.fori_loop(1, count, lambda at, _: (step(at), 0)[1], 0)
+    lax.fori_loop(1, count, lambda at, _: (step(at), 0)[1], 0)
 
 
 def kernel(sizes, scale, kr, act, grads, words_in, columns_in, begin_in, half_in, val_in, out,
@@ -60,9 +56,8 @@
     me = c * E + k
     rp, gp_len = act.shape[1], grads.shape[1]
     gh = gp_len // C
-    row_block = min(ROWS, rp)
-    halves_of = rp // row_block
-    ah = row_block // E
+    ah = rp // E
+    row_block = min(ROWS, ah)
     total_rows, total_cols = a_buf.shape[0], g_buf.shape[0]
     in_width, out_width = total_rows * C, total_cols * E
     word_count = words.shape[1]
@@ -102,40 +97,35 @@
     def g_rows(piece, part_at):
         return pl.ds(pl.multiple_of(piece * gp_len + part_at * gh, gh), gh)
 
-    def a_rows(piece, h, part_at):
-        return pl.ds(pl.multiple_of(piece * rp + h * row_block + part_at * ah, ah), ah)
+    def a_rows(piece, part_at):
+        return pl.ds(pl.multiple_of(piece * rp + part_at * ah, ah), ah)
 
     def g_send(o):
         t = lax.rem(s + o, S)
         return remote(grads.at[t, pl.ds(pl.multiple_of(c * gh, gh), gh)], g_buf.at[g_rows(s, c)],
                       gz_send.at[o], gz_recv.at[s], place(t, c, k))
 
-    def a_send(o, h):
+    def a_send(o):
         t = lax.rem(s + o, S)
-        return remote(act.at[t, pl.ds(pl.multiple_of(h * row_block + k * ah, ah), ah)],
-                      a_buf.at[a_rows(s, h, k)], az_send.at[o, h], az_recv.at[s, h],
-                      place(t, c, k))
+        return remote(act.at[t, pl.ds(pl.multiple_of(k * ah, ah), ah)], a_buf.at[a_rows(s, k)],
+                      az_send.at[o], az_recv.at[s], place(t, c, k))
 
     def g_pass(piece, m):
         return remote(g_buf.at[g_rows(piece, c)], g_buf.at[g_rows(piece, c)],
                       gx_send.at[piece, m], gx_recv.at[piece, c], place(s, lax.rem(c + m, C), k))
 
-    def a_pass(piece, h, m):
-        rows = a_rows(piece, h, k)
-        return remote(a_buf.at[rows], a_buf.at[rows], ax_send.at[piece, h, m],
-                      ax_recv.at[piece, h, k], place(s, c, lax.rem(k + m, E)))
+    def a_pass(piece, m):
+        rows = a_rows(piece, k)
+        return remote(a_buf.at[rows], a_buf.at[rows], ax_send.at[piece, m],
+                      ax_recv.at[piece, k], place(s, c, lax.rem(k + m, E)))
 
     def arrived(ref, sem):
         pltpu.make_async_copy(ref, ref, sem).wait()
 
-    started = []
-
-    def start(copy):
-        copy.start()
-        started.append(copy)
-
-    for o in range(1, S):
-        start(g_send(o))
+    def pieces(step):
+        each(S, lambda o: step(o, lax.rem(s - o + S, S)))
+
+    each(S, lambda o: g_send(o).start())
     for copy in local[3:]:
         copy.start()
 
@@ -146,19 +136,26 @@
     for q in range(Q):
         ring[me, 0:1, q * per_q:(q + 1) * per_q] = begins[...]
         ring[me, 1:2, q * per_q:(q + 1) * per_q] = halves[...]
-    for m in range(1, Q):
-        q = lax.rem(me + m, Q)
-        start(remote(ring.at[me], ring.at[me], r_send.at[m], r_recv.at[me], spot(s, q)))
+
+    def r_copy(m):
+        return remote(ring.at[me], ring.at[me], r_send.at[m], r_recv.at[me],
+                      spot(s, lax.rem(me + m, Q)))
+
+    each(Q, lambda m: r_copy(m).start())
 
     local[2].wait()
     width = out_width // kept
     kept_cols = columns[...] + iota((1, kept), 1) * width
-    for b in range(BITS):
+
+    def tabulate(b, carry):
         at = iota((word_count, kept), 0) * BITS + b
         full = ((jnp.right_shift(at, log2(gp_len)) * E + k) * gp_len
                 + jnp.bitwise_and(at, gp_len - 1))
-        table[b * word_count:(b + 1) * word_count, :] = sign_of(
+        table[pl.ds(pl.multiple_of(b * word_count, word_count), word_count), :] = sign_of(
             jnp.bitwise_and(full, kept_cols)).astype(BF16)
+        return carry
+
+    lax.fori_loop(0, BITS, tabulate, 0)
     hada[...] = sign_of(jnp.bitwise_and(
         iota((row_block, row_block), 0), iota((row_block, row_block), 1))).astype(BF16)
 
@@ -177,29 +174,39 @@
             gp[pl.ds(pl.multiple_of(b * word_count + at * block_words, block_words),
                      block_words), :] = moved[b * block_words:(b + 1) * block_words]
 
-    for o in range(1, S):
-        piece = lax.rem(s - o + S, S)
+    def g_step(o, piece):
         arrived(g_buf.at[g_rows(piece, c)], gz_recv.at[piece])
-        for h in range(halves_of):
-            start(a_send(o, h))
-        for m in range(1, C):
-            start(g_pass(piece, m))
+        a_send(o).start()
+        each(C, lambda m: g_pass(piece, m).start())
+
+    pieces(g_step)
     local[3].wait()
     piece_blocks = block == gp_len
-    if piece_blocks:
-        permute(s)
-    for o in range(1, S):
+
+    def g_whole(o, carry):
         piece = lax.rem(s - o + S, S)
-        for m in range(1, C):
-            other = lax.rem(c + m, C)
-            arrived(g_buf.at[g_rows(piece, other)], gx_recv.at[piece, other])
+
+        @pl.when(o > 0)
+        def _():
+            def wait(m):
+                other = lax.rem(c + m, C)
+                arrived(g_buf.at[g_rows(piece, other)], gx_recv.at[piece, other])
+            each(C, wait)
         if piece_blocks:
             permute(piece)
+        return carry
+
+    lax.fori_loop(0, S, g_whole, 0)
     if not piece_blocks:
         lax.fori_loop(0, blocks, lambda at, _: (permute(at), 0)[1], 0)
     wide = min(WIDE, total_cols)
-    for at in range(total_cols // wide):
-        gt[:, at * wide:(at + 1) * wide] = gp[at * wide:(at + 1) * wide, :].T
+
+    def turn(at, carry):
+        here = pl.ds(pl.multiple_of(at * wide, wide), wide)
+        gt[:, here] = gp[here, :].T
+        return carry
+
+    lax.fori_loop(0, total_cols // wide, turn, 0)
 
     def score_rows(row):
         here = pl.ds(pl.multiple_of(row, row_block), row_block)
@@ -223,17 +230,29 @@
 
     local[4].wait()
     local[5].wait()
-    lax.fori_loop(0, halves_of, lambda h, _: (score_rows(s * rp + h * row_block), 0)[1], 0)
-    for o in range(1, S):
+
+    def a_step(n, carry):
+        o, m = lax.div(n, E), lax.rem(n, E)
         piece = lax.rem(s - o + S, S)
-        for h in range(halves_of):
-            arrived(a_buf.at[a_rows(piece, h, k)], az_recv.at[piece, h])
-            for m in range(1, E):
-                start(a_pass(piece, h, m))
-            for m in range(1, E):
-                other = lax.rem(k + m, E)
-                arrived(a_buf.at[a_rows(piece, h, other)], ax_recv.at[piece, h, other])
-            score_rows(piece * rp + h * row_block)
+        other = lax.rem(k + m, E)
+
+        @pl.when(jnp.logical_and(o > 0, m == 0))
+        def _():
+            arrived(a_buf.at[a_rows(piece, k)], az_recv.at[piece])
+            each(E, lambda at: a_pass(piece, at).start())
+
+        @pl.when(jnp.logical_and(o > 0, m > 0))
+        def _():
+            arrived(a_buf.at[a_rows(piece, other)], ax_recv.at[piece, other])
+
+        def rows(at, inner):
+            score_rows(piece * rp + other * ah + at * row_block)
+            return inner
+
+        lax.fori_loop(0, ah // row_block, rows, 0)
+        return carry
+
+    lax.fori_loop(0, S * E, a_step, 0)
 
     mixed = [part[at:at + row_block, :] for at in range(0, total_rows, row_block)]
     step = 1
@@ -254,9 +273,11 @@
             turned[turned_rows:turned_rows + LANES, :] = values[b:b + LANES, :].T
             turned_rows += LANES
 
-    for m in range(1, Q):
+    def r_arrived(m):
         q = lax.rem(me + m, Q)
         arrived(ring.at[q], r_recv.at[q])
+
+    each(Q, r_arrived)
     lane = iota((1, kept), 1)
     begin = jnp.zeros((1, kept), I32)
     half = jnp.zeros((1, kept), I32)
@@ -340,14 +361,11 @@
     def e_rows(e):
         return pl.ds(pl.multiple_of(e * 8, 8), 8)
 
-    if S <= 16:
-        for e in range(S):
-            answers[e * 8:(e + 1) * 8, :] = products(e)
-    else:
-        def put(e, carry):
-            answers[e_rows(e), :] = products(e)
-            return carry
-        lax.fori_loop(0, S, put, 0)
+    def put(e, carry):
+        answers[e_rows(e), :] = products(e)
+        return carry
+
+    lax.fori_loop(0, S, put, 0)
 
     def s_copy(m):
         t, q = member(jnp.int32(m))
@@ -366,8 +384,15 @@
     for at in range(1, S * Q):
         all_sums = all_sums + sums[at]
     out[...] = all_sums[0:1, :nv] / jnp.sqrt(all_sums[0:1, nv:nv + 1] + 1e-06)
-    for copy in started:
-        copy.wait_send()
+
+    def sent(o, piece):
+        g_send(o).wait_send()
+        a_send(o).wait_send()
+        each(C, lambda m: g_pass(piece, m).wait_send())
+        each(E, lambda m: a_pass(piece, m).wait_send())
+
+    pieces(sent)
+    each(Q, lambda m: r_copy(m).wait_send())
     each(S * Q, lambda m: p_copy(m).wait_send())
     each(S * Q, lambda m: s_copy(m).wait_send())
 
@@ -384,8 +409,7 @@
     kr = keep // kept
     nv = val_sketch.shape[0] * S
     words = sign_bits.reshape(local_rows, -1)
-    row_block = min(ROWS, rp)
-    halves = rp // row_block
+    row_block = min(ROWS, rp // E)
     hbm = pl.BlockSpec(memory_space=pl.ANY)
     dma = pltpu.SemaphoreType.DMA
     block = min(WIDE, local_cols)
@@ -416,8 +440,8 @@
             pltpu.VMEM((S * Q, keep // LANES // Q, LANES), F32),
             pltpu.VMEM((S * Q, 8, LANES), F32),
             dma((7,)),
-            dma((S,)), dma((S,)), dma((S, halves)), dma((S, halves)),
-            dma((S, C)), dma((S, C)), dma((S, halves, E)), dma((S, halves, E)),
+            dma((S,)), dma((S,)), dma((S,)), dma((S,)),
+            dma((S, C)), dma((S, C)), dma((S, E)), dma((S, E)),
             dma((Q,)), dma((Q,)),
             dma((S * Q,)), dma((S * Q,)), dma((S * Q,)), dma((S * Q,)),
         ],

time: 83.7 us -> 76.9 us (0.919)
  Pallas kernels: 82.4 us -> 75.5 us
    pallas_call x1, Pallas kernels: 82.4 us -> 75.5 us  [body(): pl.pallas_call(functools.partial(kernel, (S, C, E), 1.0 / (math.sqrt(in_w...]
where the time goes in v3:
time: 76.9 us; the launch traced here: 76.7 us
  Pallas kernels  75.5 us (98%)
  local copies, waits for them, and re-layouts  1.19 us (2%)
    pallas_call x1, Pallas kernels, body(): pl.pallas_call(functools.partial(kernel, (S, C, E), 1.0 / (math.sqrt(in_w...  75.5 us

profile of v3, /device:TPU:0, one launch (start us, length us, event | category | flops | bytes accessed | tf_op | source)
XLA Modules:
  0.0 76.7 jit_solution(11411240169720938890)
XLA Ops:
  0.0 75.5 %scores.1 = f32[1,64]{1,0:T(1,128)} custom-call(bf16[4,512,512]{2,1,0:T(8,128)(2,1)} %act.1, bf16[4,512,512]{2,1,0:T(8,128)(2,1)} %grads.1, s32[2048,128]{1,0:T(8,128)} %bitcast.4, s32[1,128]{1,0:T(1,128)} %bitcast.5, s32[1,32]{1,0:T(1,128)} %bitcast.6, s32[1,32]{1,0:T(1,128)} %bitcast.7, f32[16,2048]{1,0:T(8,128)} %val_in.1), custom_call_target="tpu_custom_call" | custom-call | flops 6442450944 | bytes 4194304 | tf_op jit(solution)/shard_map/scores/pallas_call | solution.py:416
  75.6 1.2 %copy.9 = f32[1,64]{1,0:T(1,128)} copy(f32[1,64]{1,0:T(1,128)} %scores.1) | data formatting | bytes 512

commit v4 on v3

--- a/solution.py
+++ b/solution.py
@@ -16,6 +16,7 @@
 BITS = 16
 ROWS = 256
 WIDE = 512
+WINDOW = 3
 
 
 def log2(n):
@@ -42,7 +43,15 @@
 
 
 def each(count, step):
-    lax.fori_loop(1, count, lambda at, _: (step(at), 0)[1], 0)
+    if count <= 16:
+        for at in range(1, count):
+            step(at)
+    else:
+        lax.fori_loop(1, count, lambda at, _: (step(at), 0)[1], 0)
+
+
+def wrap(at, size):
+    return jnp.bitwise_and(at, size - 1)
 
 
 def kernel(sizes, scale, kr, act, grads, words_in, columns_in, begin_in, half_in, val_in, out,
@@ -56,25 +65,25 @@
     me = c * E + k
     rp, gp_len = act.shape[1], grads.shape[1]
     gh = gp_len // C
-    ah = rp // E
-    row_block = min(ROWS, ah)
+    row_block = min(ROWS, rp)
+    parts_of = rp // row_block
+    ah = row_block // E
     total_rows, total_cols = a_buf.shape[0], g_buf.shape[0]
     in_width, out_width = total_rows * C, total_cols * E
     word_count = words.shape[1]
     kept = columns.shape[1]
 
     def member(m):
-        t = lax.rem(s + lax.div(m, Q), S)
-        q = lax.rem(me + lax.rem(m, Q), Q)
-        return t, q
+        m = jnp.int32(m)
+        return wrap(s + jnp.right_shift(m, log2(Q)), S), wrap(me + m, Q)
 
     def spot(t, q):
-        return place(t, lax.div(q, E), lax.rem(q, E))
+        return place(t, jnp.right_shift(q, log2(E)), wrap(q, E))
 
     barrier = pltpu.get_barrier_semaphore()
 
     def greet(m):
-        pl.semaphore_signal(barrier, inc=1, device_id=spot(*member(jnp.int32(m))),
+        pl.semaphore_signal(barrier, inc=1, device_id=spot(*member(m)),
                             device_id_type=MESH)
 
     local = [
@@ -85,7 +94,7 @@
             (words_in, words), (val_in, val)))
     ]
     each(S * Q, greet)
-    for copy in local[:3]:
+    for copy in local:
         copy.start()
     pl.semaphore_wait(barrier, S * Q - 1)
 
@@ -97,37 +106,42 @@
     def g_rows(piece, part_at):
         return pl.ds(pl.multiple_of(piece * gp_len + part_at * gh, gh), gh)
 
-    def a_rows(piece, part_at):
-        return pl.ds(pl.multiple_of(piece * rp + part_at * ah, ah), ah)
+    def a_rows(piece, h, part_at):
+        return pl.ds(pl.multiple_of(piece * rp + h * row_block + part_at * ah, ah), ah)
+
+    def nth(n):
+        n = jnp.int32(n)
+        return 1 + jnp.right_shift(n, log2(parts_of)), wrap(n, parts_of)
 
     def g_send(o):
-        t = lax.rem(s + o, S)
+        t = wrap(s + o, S)
         return remote(grads.at[t, pl.ds(pl.multiple_of(c * gh, gh), gh)], g_buf.at[g_rows(s, c)],
                       gz_send.at[o], gz_recv.at[s], place(t, c, k))
 
-    def a_send(o):
-        t = lax.rem(s + o, S)
-        return remote(act.at[t, pl.ds(pl.multiple_of(k * ah, ah), ah)], a_buf.at[a_rows(s, k)],
-                      az_send.at[o], az_recv.at[s], place(t, c, k))
+    def a_send(n):
+        o, h = nth(n)
+        t = wrap(s + o, S)
+        return remote(act.at[t, pl.ds(pl.multiple_of(h * row_block + k * ah, ah), ah)],
+                      a_buf.at[a_rows(s, h, k)], az_send.at[n], az_recv.at[s, h],
+                      place(t, c, k))
 
     def g_pass(piece, m):
         return remote(g_buf.at[g_rows(piece, c)], g_buf.at[g_rows(piece, c)],
-                      gx_send.at[piece, m], gx_recv.at[piece, c], place(s, lax.rem(c + m, C), k))
-
-    def a_pass(piece, m):
-        rows = a_rows(piece, k)
-        return remote(a_buf.at[rows], a_buf.at[rows], ax_send.at[piece, m],
-                      ax_recv.at[piece, k], place(s, c, lax.rem(k + m, E)))
+                      gx_send.at[piece, m], gx_recv.at[piece, c], place(s, wrap(c + m, C), k))
+
+    def a_pass(piece, h, m):
+        rows = a_rows(piece, h, k)
+        return remote(a_buf.at[rows], a_buf.at[rows], ax_send.at[piece, h, m],
+                      ax_recv.at[piece, h, k], place(s, c, wrap(k + m, E)))
 
     def arrived(ref, sem):
         pltpu.make_async_copy(ref, ref, sem).wait()
 
     def pieces(step):
-        each(S, lambda o: step(o, lax.rem(s - o + S, S)))
+        each(S, lambda o: step(o, wrap(s - o + S, S)))
 
     each(S, lambda o: g_send(o).start())
-    for copy in local[3:]:
-        copy.start()
+    a_send(0).start()
 
     for copy in local[:2]:
         copy.wait()
@@ -139,7 +153,7 @@
 
     def r_copy(m):
         return remote(ring.at[me], ring.at[me], r_send.at[m], r_recv.at[me],
-                      spot(s, lax.rem(me + m, Q)))
+                      spot(s, wrap(me + m, Q)))
 
     each(Q, lambda m: r_copy(m).start())
 
@@ -176,20 +190,25 @@
 
     def g_step(o, piece):
         arrived(g_buf.at[g_rows(piece, c)], gz_recv.at[piece])
-        a_send(o).start()
         each(C, lambda m: g_pass(piece, m).start())
-
+        if isinstance(o, int) and o < min(WINDOW, a_count):
+            a_send(o).start()
+
+    a_count = (S - 1) * parts_of
     pieces(g_step)
+    if S > 16:
+        for n in range(1, min(WINDOW, a_count)):
+            a_send(n).start()
     local[3].wait()
     piece_blocks = block == gp_len
 
     def g_whole(o, carry):
-        piece = lax.rem(s - o + S, S)
+        piece = wrap(s - o + S, S)
 
         @pl.when(o > 0)
         def _():
             def wait(m):
-                other = lax.rem(c + m, C)
+                other = wrap(c + m, C)
                 arrived(g_buf.at[g_rows(piece, other)], gx_recv.at[piece, other])
             each(C, wait)
         if piece_blocks:
@@ -232,27 +251,32 @@
     local[5].wait()
 
     def a_step(n, carry):
-        o, m = lax.div(n, E), lax.rem(n, E)
-        piece = lax.rem(s - o + S, S)
-        other = lax.rem(k + m, E)
-
-        @pl.when(jnp.logical_and(o > 0, m == 0))
+        o, h = nth(n - parts_of)
+        piece = wrap(s - o + S, S)
+        n_next = n - parts_of + 1
+        o_next, h_next = nth(n_next)
+        next_piece = wrap(s - o_next + S, S)
+
+        @pl.when(jnp.logical_and(n_next >= 0, n_next < a_count))
         def _():
-            arrived(a_buf.at[a_rows(piece, k)], az_recv.at[piece])
-            each(E, lambda at: a_pass(piece, at).start())
-
-        @pl.when(jnp.logical_and(o > 0, m > 0))
+            arrived(a_buf.at[a_rows(next_piece, h_next, k)], az_recv.at[next_piece, h_next])
+            each(E, lambda m: a_pass(next_piece, h_next, m).start())
+
+        @pl.when(jnp.logical_and(n_next >= 0, n_next + WINDOW < a_count))
         def _():
-            arrived(a_buf.at[a_rows(piece, other)], ax_recv.at[piece, other])
-
-        def rows(at, inner):
-            score_rows(piece * rp + other * ah + at * row_block)
-            return inner
-
-        lax.fori_loop(0, ah // row_block, rows, 0)
+            a_send(n_next + WINDOW).start()
+
+        @pl.when(n >= parts_of)
+        def _():
+            def wait(m):
+                other = wrap(k + m, E)
+                arrived(a_buf.at[a_rows(piece, h, other)], ax_recv.at[piece, h, other])
+            each(E, wait)
+
+        score_rows(piece * rp + h * row_block)
         return carry
 
-    lax.fori_loop(0, S * E, a_step, 0)
+    lax.fori_loop(0, S * parts_of, a_step, 0)
 
     mixed = [part[at:at + row_block, :] for at in range(0, total_rows, row_block)]
     step = 1
@@ -274,7 +298,7 @@
             turned_rows += LANES
 
     def r_arrived(m):
-        q = lax.rem(me + m, Q)
+        q = wrap(me + m, Q)
         arrived(ring.at[q], r_recv.at[q])
 
     each(Q, r_arrived)
@@ -323,19 +347,25 @@
         return pl.ds(pl.multiple_of(q * per, per), per)
 
     def p_copy(m):
-        t, q = member(jnp.int32(m))
-        return remote(sketch.at[q_rows(q)], parts.at[mine_at], p_send.at[m], p_recv.at[mine_at],
+        t, q = member(m)
+        return remote(sketch.at[q_rows(q)], parts.at[mine_at], p_send.at[0], p_recv.at[0],
                       spot(t, q))
 
     each(S * Q, lambda m: p_copy(m).start())
     parts[pl.ds(mine_at, 1)] = sketch[q_rows(me), :][None]
     local[6].wait()
 
-    def p_arrived(m):
-        t, q = member(jnp.int32(m))
-        arrived(parts.at[t * Q + q], p_recv.at[t * Q + q])
-
-    each(S * Q, p_arrived)
+    def sent(o, piece):
+        g_send(o).wait_send()
+        each(C, lambda m: g_pass(piece, m).wait_send())
+        for h in range(parts_of):
+            each(E, lambda m: a_pass(piece, h, m).wait_send())
+
+    pieces(sent)
+    each(a_count + 1, lambda n: a_send(n - 1).wait_send())
+    each(Q, lambda m: r_copy(m).wait_send())
+    others = pl.ds(0, S * Q - 1)
+    arrived(parts.at[others], p_recv.at[0])
     nvl = val.shape[0]
     nv = nvl * S
     out_lane = iota((1, LANES), 1)
@@ -368,33 +398,20 @@
     lax.fori_loop(0, S, put, 0)
 
     def s_copy(m):
-        t, q = member(jnp.int32(m))
-        return remote(answers.at[e_rows(t)], sums.at[mine_at], s_send.at[m], s_recv.at[mine_at],
+        t, q = member(m)
+        return remote(answers.at[e_rows(t)], sums.at[mine_at], s_send.at[0], s_recv.at[0],
                       spot(t, q))
 
     each(S * Q, lambda m: s_copy(m).start())
     sums[pl.ds(mine_at, 1)] = answers[e_rows(s), :][None]
 
-    def s_arrived(m):
-        t, q = member(jnp.int32(m))
-        arrived(sums.at[t * Q + q], s_recv.at[t * Q + q])
-
-    each(S * Q, s_arrived)
+    arrived(sums.at[others], s_recv.at[0])
     all_sums = sums[0]
     for at in range(1, S * Q):
         all_sums = all_sums + sums[at]
     out[...] = all_sums[0:1, :nv] / jnp.sqrt(all_sums[0:1, nv:nv + 1] + 1e-06)
-
-    def sent(o, piece):
-        g_send(o).wait_send()
-        a_send(o).wait_send()
-        each(C, lambda m: g_pass(piece, m).wait_send())
-        each(E, lambda m: a_pass(piece, m).wait_send())
-
-    pieces(sent)
-    each(Q, lambda m: r_copy(m).wait_send())
-    each(S * Q, lambda m: p_copy(m).wait_send())
-    each(S * Q, lambda m: s_copy(m).wait_send())
+    arrived(parts.at[others], p_send.at[0])
+    arrived(sums.at[others], s_send.at[0])
 
 
 def body(activations, out_grads, sign_bits, keep_cols, row_start, row_step, val_sketch):
@@ -409,7 +426,9 @@
     kr = keep // kept
     nv = val_sketch.shape[0] * S
     words = sign_bits.reshape(local_rows, -1)
-    row_block = min(ROWS, rp // E)
+    row_block = min(ROWS, rp)
+    parts_of = rp // row_block
+    a_count = (S - 1) * parts_of
     hbm = pl.BlockSpec(memory_space=pl.ANY)
     dma = pltpu.SemaphoreType.DMA
     block = min(WIDE, local_cols)
@@ -440,10 +459,10 @@
             pltpu.VMEM((S * Q, keep // LANES // Q, LANES), F32),
             pltpu.VMEM((S * Q, 8, LANES), F32),
             dma((7,)),
-            dma((S,)), dma((S,)), dma((S,)), dma((S,)),
-            dma((S, C)), dma((S, C)), dma((S, E)), dma((S, E)),
+            dma((S,)), dma((S,)), dma((a_count,)), dma((S, parts_of)),
+            dma((S, C)), dma((S, C)), dma((S, parts_of, E)), dma((S, parts_of, E)),
             dma((Q,)), dma((Q,)),
-            dma((S * Q,)), dma((S * Q,)), dma((S * Q,)), dma((S * Q,)),
+            dma((1,)), dma((1,)), dma((1,)), dma((1,)),
         ],
         compiler_params=pltpu.CompilerParams(
             collective_id=0, has_side_effects=True, vmem_limit_bytes=60 * 2**20),

time: 76.9 us -> 74.8 us (0.973)
  Pallas kernels: 75.5 us -> 73.5 us
    pallas_call x1, Pallas kernels: 75.5 us -> 73.5 us  [body(): pl.pallas_call(functools.partial(kernel, (S, C, E), 1.0 / (math.sqrt(in_w...]
where the time goes in v4:
time: 74.8 us; the launch traced here: 74.7 us
  Pallas kernels  73.5 us (98%)
  local copies, waits for them, and re-layouts  1.19 us (2%)
    pallas_call x1, Pallas kernels, body(): pl.pallas_call(functools.partial(kernel, (S, C, E), 1.0 / (math.sqrt(in_w...  73.5 us

profile of v4, /device:TPU:0, one launch (start us, length us, event | category | flops | bytes accessed | tf_op | source)
XLA Modules:
  0.0 74.7 jit_solution(7231422818765856401)
XLA Ops:
  0.0 73.5 %scores.1 = f32[1,64]{1,0:T(1,128)} custom-call(bf16[4,512,512]{2,1,0:T(8,128)(2,1)} %act.1, bf16[4,512,512]{2,1,0:T(8,128)(2,1)} %grads.1, s32[2048,128]{1,0:T(8,128)} %bitcast.4, s32[1,128]{1,0:T(1,128)} %bitcast.5, s32[1,32]{1,0:T(1,128)} %bitcast.6, s32[1,32]{1,0:T(1,128)} %bitcast.7, f32[16,2048]{1,0:T(8,128)} %val_in.1), custom_call_target="tpu_custom_call" | custom-call | flops 6442450944 | bytes 4194304 | tf_op jit(solution)/shard_map/scores/pallas_call | solution.py:435
  73.5 1.2 %copy.9 = f32[1,64]{1,0:T(1,128)} copy(f32[1,64]{1,0:T(1,128)} %scores.1) | data formatting | bytes 512

commit v5 on v4

--- a/solution.py
+++ b/solution.py
@@ -16,7 +16,7 @@
 BITS = 16
 ROWS = 256
 WIDE = 512
-WINDOW = 3
+WINDOW = 4
 
 
 def log2(n):
@@ -65,6 +65,8 @@
     me = c * E + k
     rp, gp_len = act.shape[1], grads.shape[1]
     gh = gp_len // C
+    g_parts = 2 if gh % 64 == 0 else 1
+    gq = gh // g_parts
     row_block = min(ROWS, rp)
     parts_of = rp // row_block
     ah = row_block // E
@@ -103,31 +105,36 @@
             src_ref=src, dst_ref=dst, send_sem=send, recv_sem=recv,
             device_id=target, device_id_type=MESH)
 
-    def g_rows(piece, part_at):
-        return pl.ds(pl.multiple_of(piece * gp_len + part_at * gh, gh), gh)
+    g_count, a_count = (S - 1) * g_parts, (S - 1) * parts_of
+
+    def g_rows(piece, h, part_at):
+        return pl.ds(pl.multiple_of(piece * gp_len + part_at * gh + h * gq, gq), gq)
 
     def a_rows(piece, h, part_at):
         return pl.ds(pl.multiple_of(piece * rp + h * row_block + part_at * ah, ah), ah)
 
-    def nth(n):
+    def nth(n, parts_in):
         n = jnp.int32(n)
-        return 1 + jnp.right_shift(n, log2(parts_of)), wrap(n, parts_of)
-
-    def g_send(o):
+        return 1 + jnp.right_shift(n, log2(parts_in)), wrap(n, parts_in)
+
+    def g_send(n):
+        o, h = nth(n, g_parts)
         t = wrap(s + o, S)
-        return remote(grads.at[t, pl.ds(pl.multiple_of(c * gh, gh), gh)], g_buf.at[g_rows(s, c)],
-                      gz_send.at[o], gz_recv.at[s], place(t, c, k))
+        return remote(grads.at[t, pl.ds(pl.multiple_of(c * gh + h * gq, gq), gq)],
+                      g_buf.at[g_rows(s, h, c)], gz_send.at[n], gz_recv.at[s, h],
+                      place(t, c, k))
 
     def a_send(n):
-        o, h = nth(n)
+        o, h = nth(n, parts_of)
         t = wrap(s + o, S)
         return remote(act.at[t, pl.ds(pl.multiple_of(h * row_block + k * ah, ah), ah)],
                       a_buf.at[a_rows(s, h, k)], az_send.at[n], az_recv.at[s, h],
                       place(t, c, k))
 
-    def g_pass(piece, m):
-        return remote(g_buf.at[g_rows(piece, c)], g_buf.at[g_rows(piece, c)],
-                      gx_send.at[piece, m], gx_recv.at[piece, c], place(s, wrap(c + m, C), k))
+    def g_pass(piece, h, m):
+        rows = g_rows(piece, h, c)
+        return remote(g_buf.at[rows], g_buf.at[rows], gx_send.at[piece, h, m],
+                      gx_recv.at[piece, h, c], place(s, wrap(c + m, C), k))
 
     def a_pass(piece, h, m):
         rows = a_rows(piece, h, k)
@@ -140,8 +147,18 @@
     def pieces(step):
         each(S, lambda o: step(o, wrap(s - o + S, S)))
 
-    each(S, lambda o: g_send(o).start())
-    a_send(0).start()
+    def issue(n):
+        n = jnp.int32(n)
+
+        @pl.when(n < g_count)
+        def _():
+            g_send(n).start()
+
+        @pl.when(jnp.logical_and(n >= g_count, n < g_count + a_count))
+        def _():
+            a_send(n - g_count).start()
+
+    lax.fori_loop(0, WINDOW, lambda n, _: (issue(n), 0)[1], 0)
 
     for copy in local[:2]:
         copy.wait()
@@ -188,34 +205,35 @@
             gp[pl.ds(pl.multiple_of(b * word_count + at * block_words, block_words),
                      block_words), :] = moved[b * block_words:(b + 1) * block_words]
 
-    def g_step(o, piece):
-        arrived(g_buf.at[g_rows(piece, c)], gz_recv.at[piece])
-        each(C, lambda m: g_pass(piece, m).start())
-        if isinstance(o, int) and o < min(WINDOW, a_count):
-            a_send(o).start()
-
-    a_count = (S - 1) * parts_of
-    pieces(g_step)
-    if S > 16:
-        for n in range(1, min(WINDOW, a_count)):
-            a_send(n).start()
-    local[3].wait()
     piece_blocks = block == gp_len
 
-    def g_whole(o, carry):
+    def g_whole(o):
         piece = wrap(s - o + S, S)
-
-        @pl.when(o > 0)
-        def _():
+        for h in range(g_parts):
             def wait(m):
                 other = wrap(c + m, C)
-                arrived(g_buf.at[g_rows(piece, other)], gx_recv.at[piece, other])
+                arrived(g_buf.at[g_rows(piece, h, other)], gx_recv.at[piece, h, other])
             each(C, wait)
         if piece_blocks:
             permute(piece)
+
+    def g_step(n, carry):
+        o, h = nth(n, g_parts)
+        piece = wrap(s - o + S, S)
+        arrived(g_buf.at[g_rows(piece, h, c)], gz_recv.at[piece, h])
+        each(C, lambda m: g_pass(piece, h, m).start())
+        issue(n + WINDOW)
+
+        @pl.when(jnp.logical_and(h == 0, o > 1))
+        def _():
+            g_whole(o - 1)
         return carry
 
-    lax.fori_loop(0, S, g_whole, 0)
+    local[3].wait()
+    if piece_blocks:
+        permute(s)
+    lax.fori_loop(0, g_count, g_step, 0)
+    g_whole(jnp.int32(S - 1))
     if not piece_blocks:
         lax.fori_loop(0, blocks, lambda at, _: (permute(at), 0)[1], 0)
     wide = min(WIDE, total_cols)
@@ -251,20 +269,17 @@
     local[5].wait()
 
     def a_step(n, carry):
-        o, h = nth(n - parts_of)
+        o, h = nth(n - parts_of, parts_of)
         piece = wrap(s - o + S, S)
         n_next = n - parts_of + 1
-        o_next, h_next = nth(n_next)
+        o_next, h_next = nth(n_next, parts_of)
         next_piece = wrap(s - o_next + S, S)
 
         @pl.when(jnp.logical_and(n_next >= 0, n_next < a_count))
         def _():
             arrived(a_buf.at[a_rows(next_piece, h_next, k)], az_recv.at[next_piece, h_next])
             each(E, lambda m: a_pass(next_piece, h_next, m).start())
-
-        @pl.when(jnp.logical_and(n_next >= 0, n_next + WINDOW < a_count))
-        def _():
-            a_send(n_next + WINDOW).start()
+            issue(g_count + n_next + WINDOW)
 
         @pl.when(n >= parts_of)
         def _():
@@ -356,12 +371,13 @@
     local[6].wait()
 
     def sent(o, piece):
-        g_send(o).wait_send()
-        each(C, lambda m: g_pass(piece, m).wait_send())
+        for h in range(g_parts):
+            each(C, lambda m: g_pass(piece, h, m).wait_send())
         for h in range(parts_of):
             each(E, lambda m: a_pass(piece, h, m).wait_send())
 
     pieces(sent)
+    each(g_count + 1, lambda n: g_send(n - 1).wait_send())
     each(a_count + 1, lambda n: a_send(n - 1).wait_send())
     each(Q, lambda m: r_copy(m).wait_send())
     others = pl.ds(0, S * Q - 1)
@@ -429,6 +445,8 @@
     row_block = min(ROWS, rp)
     parts_of = rp // row_block
     a_count = (S - 1) * parts_of
+    g_parts = 2 if (gp_len // C) % 64 == 0 else 1
+    g_count = (S - 1) * g_parts
     hbm = pl.BlockSpec(memory_space=pl.ANY)
     dma = pltpu.SemaphoreType.DMA
     block = min(WIDE, local_cols)
@@ -459,8 +477,9 @@
             pltpu.VMEM((S * Q, keep // LANES // Q, LANES), F32),
             pltpu.VMEM((S * Q, 8, LANES), F32),
             dma((7,)),
-            dma((S,)), dma((S,)), dma((a_count,)), dma((S, parts_of)),
-            dma((S, C)), dma((S, C)), dma((S, parts_of, E)), dma((S, parts_of, E)),
+            dma((g_count,)), dma((S, g_parts)), dma((a_count,)), dma((S, parts_of)),
+            dma((S, g_parts, C)), dma((S, g_parts, C)),
+            dma((S, parts_of, E)), dma((S, parts_of, E)),
             dma((Q,)), dma((Q,)),
             dma((1,)), dma((1,)), dma((1,)), dma((1,)),
         ],

time: 74.8 us -> 72.8 us (0.973)
  Pallas kernels: 73.5 us -> 71.5 us
    pallas_call x1, Pallas kernels: 73.5 us -> 71.5 us  [body(): pl.pallas_call(functools.partial(kernel, (S, C, E), 1.0 / (math.sqrt(in_w...]
where the time goes in v5:
time: 72.8 us; the launch traced here: 72.7 us
  Pallas kernels  71.5 us (98%)
  local copies, waits for them, and re-layouts  1.19 us (2%)
    pallas_call x1, Pallas kernels, body(): pl.pallas_call(functools.partial(kernel, (S, C, E), 1.0 / (math.sqrt(in_w...  71.5 us

profile of v5, /device:TPU:0, one launch (start us, length us, event | category | flops | bytes accessed | tf_op | source)
XLA Modules:
  0.0 72.7 jit_solution(12418911733899353720)
XLA Ops:
  0.0 71.5 %scores.1 = f32[1,64]{1,0:T(1,128)} custom-call(bf16[4,512,512]{2,1,0:T(8,128)(2,1)} %act.1, bf16[4,512,512]{2,1,0:T(8,128)(2,1)} %grads.1, s32[2048,128]{1,0:T(8,128)} %bitcast.4, s32[1,128]{1,0:T(1,128)} %bitcast.5, s32[1,32]{1,0:T(1,128)} %bitcast.6, s32[1,32]{1,0:T(1,128)} %bitcast.7, f32[16,2048]{1,0:T(8,128)} %val_in.1), custom_call_target="tpu_custom_call" | custom-call | flops 6442450944 | bytes 4194304 | tf_op jit(solution)/shard_map/scores/pallas_call | solution.py:453
  71.5 1.2 %copy.9 = f32[1,64]{1,0:T(1,128)} copy(f32[1,64]{1,0:T(1,128)} %scores.1) | data formatting | bytes 512

commit v6 on v5

--- a/solution.py
+++ b/solution.py
@@ -16,7 +16,7 @@
 BITS = 16
 ROWS = 256
 WIDE = 512
-WINDOW = 4
+WINDOW = 6
 
 
 def log2(n):
@@ -113,20 +113,23 @@
     def a_rows(piece, h, part_at):
         return pl.ds(pl.multiple_of(piece * rp + h * row_block + part_at * ah, ah), ah)
 
+    def mate(n):
+        far = S // 2 + jnp.right_shift(n, 1)
+        near = jnp.right_shift(n + 1, 1)
+        return jnp.bitwise_xor(s, jnp.where(jnp.bitwise_and(n, 1) == 0, far, near))
+
     def nth(n, parts_in):
         n = jnp.int32(n)
-        return 1 + jnp.right_shift(n, log2(parts_in)), wrap(n, parts_in)
+        return mate(jnp.right_shift(n, log2(parts_in))), wrap(n, parts_in)
 
     def g_send(n):
-        o, h = nth(n, g_parts)
-        t = wrap(s + o, S)
+        t, h = nth(n, g_parts)
         return remote(grads.at[t, pl.ds(pl.multiple_of(c * gh + h * gq, gq), gq)],
                       g_buf.at[g_rows(s, h, c)], gz_send.at[n], gz_recv.at[s, h],
                       place(t, c, k))
 
     def a_send(n):
-        o, h = nth(n, parts_of)
-        t = wrap(s + o, S)
+        t, h = nth(n, parts_of)
         return remote(act.at[t, pl.ds(pl.multiple_of(h * row_block + k * ah, ah), ah)],
                       a_buf.at[a_rows(s, h, k)], az_send.at[n], az_recv.at[s, h],
                       place(t, c, k))
@@ -145,7 +148,7 @@
         pltpu.make_async_copy(ref, ref, sem).wait()
 
     def pieces(step):
-        each(S, lambda o: step(o, wrap(s - o + S, S)))
+        each(S, lambda o: step(mate(jnp.int32(o - 1))))
 
     def issue(n):
         n = jnp.int32(n)
@@ -207,8 +210,8 @@
 
     piece_blocks = block == gp_len
 
-    def g_whole(o):
-        piece = wrap(s - o + S, S)
+    def g_whole(n):
+        piece = mate(n)
         for h in range(g_parts):
             def wait(m):
                 other = wrap(c + m, C)
@@ -218,22 +221,54 @@
             permute(piece)
 
     def g_step(n, carry):
-        o, h = nth(n, g_parts)
-        piece = wrap(s - o + S, S)
+        piece, h = nth(n, g_parts)
         arrived(g_buf.at[g_rows(piece, h, c)], gz_recv.at[piece, h])
         each(C, lambda m: g_pass(piece, h, m).start())
         issue(n + WINDOW)
 
-        @pl.when(jnp.logical_and(h == 0, o > 1))
+        @pl.when(jnp.logical_and(h == 0, n > 0))
         def _():
-            g_whole(o - 1)
+            g_whole(jnp.right_shift(n, log2(g_parts)) - 1)
         return carry
 
+    def r_arrived(m):
+        q = wrap(me + m, Q)
+        arrived(ring.at[q], r_recv.at[q])
+
+    each(Q, r_arrived)
+    lane = iota((1, kept), 1)
+    begin = jnp.zeros((1, kept), I32)
+    half = jnp.zeros((1, kept), I32)
+    for q in range(Q):
+        mine = jnp.right_shift(lane, log2(per_q)) == q
+        begin = jnp.where(mine, ring[q, 0:1, :], begin)
+        half = jnp.where(mine, ring[q, 1:2, :], half)
+    fold = LANES // kr
+    high_rows = kept // fold
+    shape = (high_rows, LANES)
+    wide_lane = iota(shape, 1)
+    at_i = jnp.bitwise_and(wide_lane, kr - 1)
+    group = jnp.right_shift(wide_lane, log2(kr))
+
+    def down(vector):
+        plain[...] = jnp.broadcast_to(vector, (kept, kept)).T
+        got = plain[pl.ds(0, high_rows, stride=fold), :]
+        for f in range(1, fold):
+            got = jnp.where(group == f, plain[pl.ds(f, high_rows, stride=fold), :], got)
+        return got
+
+    row = jnp.bitwise_and(down(begin) + at_i * (2 * down(half) + 1), in_width - 1)
+    piece_bits, context_bits = log2(rp), log2(C)
+    sign = sign_of(jnp.bitwise_and(jnp.bitwise_and(jnp.right_shift(row, piece_bits), C - 1), c))
+    held = (jnp.left_shift(jnp.right_shift(row, piece_bits + context_bits), piece_bits)
+            + jnp.bitwise_and(row, rp - 1))
+    in_block = jnp.bitwise_and(held, LANES - 1)
+    which = jnp.right_shift(held, log2(LANES))
     local[3].wait()
     if piece_blocks:
         permute(s)
     lax.fori_loop(0, g_count, g_step, 0)
-    g_whole(jnp.int32(S - 1))
+    g_whole(jnp.int32(S - 2))
     if not piece_blocks:
         lax.fori_loop(0, blocks, lambda at, _: (permute(at), 0)[1], 0)
     wide = min(WIDE, total_cols)
@@ -269,11 +304,9 @@
     local[5].wait()
 
     def a_step(n, carry):
-        o, h = nth(n - parts_of, parts_of)
-        piece = wrap(s - o + S, S)
+        piece, h = nth(n - parts_of, parts_of)
         n_next = n - parts_of + 1
-        o_next, h_next = nth(n_next, parts_of)
-        next_piece = wrap(s - o_next + S, S)
+        next_piece, h_next = nth(n_next, parts_of)
 
         @pl.when(jnp.logical_and(n_next >= 0, n_next < a_count))
         def _():
@@ -312,39 +345,6 @@
             turned[turned_rows:turned_rows + LANES, :] = values[b:b + LANES, :].T
             turned_rows += LANES
 
-    def r_arrived(m):
-        q = wrap(me + m, Q)
-        arrived(ring.at[q], r_recv.at[q])
-
-    each(Q, r_arrived)
-    lane = iota((1, kept), 1)
-    begin = jnp.zeros((1, kept), I32)
-    half = jnp.zeros((1, kept), I32)
-    for q in range(Q):
-        mine = jnp.right_shift(lane, log2(per_q)) == q
-        begin = jnp.where(mine, ring[q, 0:1, :], begin)
-        half = jnp.where(mine, ring[q, 1:2, :], half)
-    fold = LANES // kr
-    high_rows = kept // fold
-    shape = (high_rows, LANES)
-    wide_lane = iota(shape, 1)
-    at_i = jnp.bitwise_and(wide_lane, kr - 1)
-    group = jnp.right_shift(wide_lane, log2(kr))
-
-    def down(vector):
-        plain[...] = jnp.broadcast_to(vector, (kept, kept)).T
-        got = plain[pl.ds(0, high_rows, stride=fold), :]
-        for f in range(1, fold):
-            got = jnp.where(group == f, plain[pl.ds(f, high_rows, stride=fold), :], got)
-        return got
-
-    row = jnp.bitwise_and(down(begin) + at_i * (2 * down(half) + 1), in_width - 1)
-    piece_bits, context_bits = log2(rp), log2(C)
-    sign = sign_of(jnp.bitwise_and(jnp.bitwise_and(jnp.right_shift(row, piece_bits), C - 1), c))
-    held = (jnp.left_shift(jnp.right_shift(row, piece_bits + context_bits), piece_bits)
-            + jnp.bitwise_and(row, rp - 1))
-    in_block = jnp.bitwise_and(held, LANES - 1)
-    which = jnp.right_shift(held, log2(LANES))
     picked = jnp.zeros(shape, F32)
     for at in range(total_rows // LANES):
         found = None
@@ -370,7 +370,7 @@
     parts[pl.ds(mine_at, 1)] = sketch[q_rows(me), :][None]
     local[6].wait()
 
-    def sent(o, piece):
+    def sent(piece):
         for h in range(g_parts):
             each(C, lambda m: g_pass(piece, h, m).wait_send())
         for h in range(parts_of):

time: 72.8 us -> 72 us (0.989)
  Pallas kernels: 71.5 us -> 70.6 us
    pallas_call x1, Pallas kernels: 71.5 us -> 70.6 us  [body(): pl.pallas_call(functools.partial(kernel, (S, C, E), 1.0 / (math.sqrt(in_w...]
where the time goes in v6:
time: 72 us; the launch traced here: 71.8 us
  Pallas kernels  70.6 us (98%)
  local copies, waits for them, and re-layouts  1.19 us (2%)
    pallas_call x1, Pallas kernels, body(): pl.pallas_call(functools.partial(kernel, (S, C, E), 1.0 / (math.sqrt(in_w...  70.6 us

profile of v6, /device:TPU:0, one launch (start us, length us, event | category | flops | bytes accessed | tf_op | source)
XLA Modules:
  0.0 71.8 jit_solution(14999743173376190119)
XLA Ops:
  0.0 70.6 %scores.1 = f32[1,64]{1,0:T(1,128)} custom-call(bf16[4,512,512]{2,1,0:T(8,128)(2,1)} %act.1, bf16[4,512,512]{2,1,0:T(8,128)(2,1)} %grads.1, s32[2048,128]{1,0:T(8,128)} %bitcast.4, s32[1,128]{1,0:T(1,128)} %bitcast.5, s32[1,32]{1,0:T(1,128)} %bitcast.6, s32[1,32]{1,0:T(1,128)} %bitcast.7, f32[16,2048]{1,0:T(8,128)} %val_in.1), custom_call_target="tpu_custom_call" | custom-call | flops 6442450944 | bytes 4194304 | tf_op jit(solution)/shard_map/scores/pallas_call | solution.py:453
  70.6 1.2 %copy.9 = f32[1,64]{1,0:T(1,128)} copy(f32[1,64]{1,0:T(1,128)} %scores.1) | data formatting | bytes 512

commit v7 on v6

--- a/solution.py
+++ b/solution.py
@@ -55,7 +55,7 @@
 
 
 def kernel(sizes, scale, kr, act, grads, words_in, columns_in, begin_in, half_in, val_in, out,
-           a_buf, g_buf, gp, gt, table, perm, hada, words, columns, begins, halves, val,
+           a_buf, g_buf, gp, gt, table, perm, hada, signs, words, columns, begins, halves, val,
            part, turned, plain, ring, sketch, parts, sums,
            own_sem, gz_send, gz_recv, az_send, az_recv, gx_send, gx_recv, ax_send, ax_recv,
            r_send, r_recv, p_send, p_recv, s_send, s_recv):
@@ -264,6 +264,17 @@
             + jnp.bitwise_and(row, rp - 1))
     in_block = jnp.bitwise_and(held, LANES - 1)
     which = jnp.right_shift(held, log2(LANES))
+    local[5].wait()
+
+    def expand(at, carry):
+        here = pl.ds(pl.multiple_of(at * row_block, row_block), row_block)
+        w = words[here, :]
+        for b in range(BITS):
+            signs[here, b * word_count:(b + 1) * word_count] = jnp.where(
+                jnp.bitwise_and(w, 1 << b) != 0, -1.0, 1.0).astype(BF16)
+        return carry
+
+    lax.fori_loop(0, total_rows // row_block, expand, 0)
     local[3].wait()
     if piece_blocks:
         permute(s)
@@ -283,16 +294,12 @@
     def score_rows(row):
         here = pl.ds(pl.multiple_of(row, row_block), row_block)
         a = a_buf[here, :]
-        w = words[here, :]
         total = jnp.zeros((row_block, kept), F32)
         for at in range(total_cols // wide):
             grad = jnp.dot(a, gt[:, at * wide:(at + 1) * wide], preferred_element_type=F32)
-            signed = []
-            for bb in range(wide // word_count):
-                bit = 1 << (at * (wide // word_count) + bb)
-                one = grad[:, bb * word_count:(bb + 1) * word_count]
-                signed.append(jnp.where(jnp.bitwise_and(w, bit) != 0, -one, one))
-            high, low = split(jnp.concatenate(signed, axis=1))
+            high, low = split(grad)
+            sign_here = signs[here, at * wide:(at + 1) * wide]
+            high, low = high * sign_here, low * sign_here
             side = table[at * wide:(at + 1) * wide, :]
             total = total + jnp.dot(high, side, preferred_element_type=F32)
             total = total + jnp.dot(low, side, preferred_element_type=F32)
@@ -301,7 +308,6 @@
         part[here, :] = got[:, :kept] + got[:, kept:]
 
     local[4].wait()
-    local[5].wait()
 
     def a_step(n, carry):
         piece, h = nth(n - parts_of, parts_of)
@@ -464,6 +470,7 @@
             pltpu.VMEM((local_cols, kept), BF16),
             pltpu.VMEM((block, block), BF16),
             pltpu.VMEM((row_block, row_block), BF16),
+            pltpu.VMEM((local_rows, local_cols), BF16),
             pltpu.VMEM(words.shape, I32),
             pltpu.VMEM((1, kept), I32),
             pltpu.VMEM((1, kept // Q), I32),

time: 72 us -> 71.9 us (level)
  no operation moved by 1% of the time
where the time goes in v7:
time: 71.9 us; the launch traced here: 71.8 us
  Pallas kernels  70.6 us (98%)
  local copies, waits for them, and re-layouts  1.19 us (2%)
    pallas_call x1, Pallas kernels, body(): pl.pallas_call(functools.partial(kernel, (S, C, E), 1.0 / (math.sqrt(in_w...  70.6 us

profile of v7, /device:TPU:0, one launch (start us, length us, event | category | flops | bytes accessed | tf_op | source)
XLA Modules:
  0.0 71.8 jit_solution(9524961790148803280)
XLA Ops:
  0.0 70.6 %scores.1 = f32[1,64]{1,0:T(1,128)} custom-call(bf16[4,512,512]{2,1,0:T(8,128)(2,1)} %act.1, bf16[4,512,512]{2,1,0:T(8,128)(2,1)} %grads.1, s32[2048,128]{1,0:T(8,128)} %bitcast.4, s32[1,128]{1,0:T(1,128)} %bitcast.5, s32[1,32]{1,0:T(1,128)} %bitcast.6, s32[1,32]{1,0:T(1,128)} %bitcast.7, f32[16,2048]{1,0:T(8,128)} %val_in.1), custom_call_target="tpu_custom_call" | custom-call | flops 6442450944 | bytes 4194304 | tf_op jit(solution)/shard_map/scores/pallas_call | solution.py:459
  70.6 1.2 %copy.9 = f32[1,64]{1,0:T(1,128)} copy(f32[1,64]{1,0:T(1,128)} %scores.1) | data formatting | bytes 512

commit v8 on v7

--- a/solution.py
+++ b/solution.py
@@ -56,7 +56,7 @@
 
 def kernel(sizes, scale, kr, act, grads, words_in, columns_in, begin_in, half_in, val_in, out,
            a_buf, g_buf, gp, gt, table, perm, hada, signs, words, columns, begins, halves, val,
-           part, turned, plain, ring, sketch, parts, sums,
+           turned, plain, ring, sketch, parts, sums,
            own_sem, gz_send, gz_recv, az_send, az_recv, gx_send, gx_recv, ax_send, ax_recv,
            r_send, r_recv, p_send, p_recv, s_send, s_recv):
     S, C, E = sizes
@@ -262,8 +262,6 @@
     sign = sign_of(jnp.bitwise_and(jnp.bitwise_and(jnp.right_shift(row, piece_bits), C - 1), c))
     held = (jnp.left_shift(jnp.right_shift(row, piece_bits + context_bits), piece_bits)
             + jnp.bitwise_and(row, rp - 1))
-    in_block = jnp.bitwise_and(held, LANES - 1)
-    which = jnp.right_shift(held, log2(LANES))
     local[5].wait()
 
     def expand(at, carry):
@@ -290,6 +288,28 @@
         return carry
 
     lax.fori_loop(0, total_cols // wide, turn, 0)
+
+    low_at = jnp.bitwise_and(held, row_block - 1)
+    high_at = jnp.right_shift(held, log2(row_block))
+    in_turn = jnp.bitwise_and(low_at, LANES - 1)
+    which = jnp.right_shift(low_at, log2(LANES))
+    sketch[...] = jnp.zeros(shape, F32)
+
+    def add_block(at, values):
+        if row_block < LANES:
+            values = jnp.concatenate(
+                [values, jnp.zeros((LANES - row_block, kept), F32)], axis=0)
+        picked = jnp.zeros(shape, F32)
+        for b in range(values.shape[0] // LANES):
+            turned[b * LANES:(b + 1) * LANES, :] = values[b * LANES:(b + 1) * LANES, :].T
+            found = None
+            for f in range(fold):
+                got = jnp.take_along_axis(
+                    turned[pl.ds(b * LANES + f, high_rows, stride=fold), :], in_turn,
+                    axis=1, mode="promise_in_bounds")
+                found = got if found is None else jnp.where(group == f, got, found)
+            picked = jnp.where(which == b, found, picked)
+        sketch[...] += picked * sign_of(jnp.bitwise_and(high_at, at))
 
     def score_rows(row):
         here = pl.ds(pl.multiple_of(row, row_block), row_block)
@@ -305,7 +325,7 @@
             total = total + jnp.dot(low, side, preferred_element_type=F32)
         got = jnp.dot(hada[...], jnp.concatenate(split(total), axis=1),
                       preferred_element_type=F32)
-        part[here, :] = got[:, :kept] + got[:, kept:]
+        add_block(jnp.right_shift(row, log2(row_block)), got[:, :kept] + got[:, kept:])
 
     local[4].wait()
 
@@ -332,34 +352,7 @@
 
     lax.fori_loop(0, S * parts_of, a_step, 0)
 
-    mixed = [part[at:at + row_block, :] for at in range(0, total_rows, row_block)]
-    step = 1
-    while step < len(mixed):
-        nxt = list(mixed)
-        for at in range(len(mixed)):
-            if at & step == 0:
-                nxt[at] = mixed[at] + mixed[at + step]
-                nxt[at + step] = mixed[at] - mixed[at + step]
-        mixed = nxt
-        step *= 2
-    whole = mixed if row_block >= LANES else [
-        jnp.concatenate(mixed[at:at + LANES // row_block], axis=0)
-        for at in range(0, len(mixed), LANES // row_block)]
-    turned_rows = 0
-    for values in whole:
-        for b in range(0, values.shape[0], LANES):
-            turned[turned_rows:turned_rows + LANES, :] = values[b:b + LANES, :].T
-            turned_rows += LANES
-
-    picked = jnp.zeros(shape, F32)
-    for at in range(total_rows // LANES):
-        found = None
-        for f in range(fold):
-            values = turned[pl.ds(at * LANES + f, high_rows, stride=fold), :]
-            got = jnp.take_along_axis(values, in_block, axis=1, mode="promise_in_bounds")
-            found = got if found is None else jnp.where(group == f, got, found)
-        picked = jnp.where(which == at, found, picked)
-    sketch[...] = picked * sign * scale
+    sketch[...] = sketch[...] * sign * scale
 
     per = high_rows // Q
     mine_at = s * Q + me
@@ -390,48 +383,40 @@
     arrived(parts.at[others], p_recv.at[0])
     nvl = val.shape[0]
     nv = nvl * S
-    out_lane = iota((1, LANES), 1)
-
-    def products(e):
+    totals, squares = [], []
+    for e in range(S):
         own = parts[e * Q]
         for q in range(1, Q):
             own = own + parts[e * Q + q]
         total = jnp.zeros((nvl, LANES), F32)
         for r in range(per):
             total = total + val[:, r * LANES:(r + 1) * LANES] * own[r:r + 1, :]
-        squares = jnp.sum(own * own, axis=0, keepdims=True)
-        tall = jnp.concatenate(
-            [total, squares, jnp.zeros((LANES - nvl - 1, LANES), F32)], axis=0)
-        line = jnp.sum(tall.T, axis=0, keepdims=True)
-        norm = jnp.sum(squares, axis=1, keepdims=True)
-        mine = pltpu.roll(jnp.where(out_lane < nvl, line, 0.0), s * nvl, axis=1)
-        mine = jnp.where(out_lane == nv, norm * (s == 0).astype(F32), mine)
-        return jnp.broadcast_to(mine, (8, LANES))
-
-    answers = part
-
-    def e_rows(e):
-        return pl.ds(pl.multiple_of(e * 8, 8), 8)
-
-    def put(e, carry):
-        answers[e_rows(e), :] = products(e)
-        return carry
-
-    lax.fori_loop(0, S, put, 0)
+        totals.append(total)
+        squares.append(jnp.sum(own * own, axis=0, keepdims=True))
+    tall = jnp.concatenate(
+        totals + squares + [jnp.zeros((LANES - nv - S, LANES), F32)], axis=0)
+    line = jnp.sum(tall.T, axis=0, keepdims=True)
+    sums[pl.ds(mine_at, 1)] = jnp.broadcast_to(line, (8, LANES))[None]
 
     def s_copy(m):
         t, q = member(m)
-        return remote(answers.at[e_rows(t)], sums.at[mine_at], s_send.at[0], s_recv.at[0],
+        return remote(sums.at[mine_at], sums.at[mine_at], s_send.at[0], s_recv.at[0],
                       spot(t, q))
 
     each(S * Q, lambda m: s_copy(m).start())
-    sums[pl.ds(mine_at, 1)] = answers[e_rows(s), :][None]
 
     arrived(sums.at[others], s_recv.at[0])
-    all_sums = sums[0]
-    for at in range(1, S * Q):
-        all_sums = all_sums + sums[at]
-    out[...] = all_sums[0:1, :nv] / jnp.sqrt(all_sums[0:1, nv:nv + 1] + 1e-06)
+    norm = None
+    for t in range(S):
+        line = sums[t * Q]
+        for q in range(1, Q):
+            line = line + sums[t * Q + q]
+        if t == 0:
+            at_norm = iota((1, LANES), 1) == nv + s
+            norm = jnp.sum(jnp.where(at_norm, line[0:1, :], 0.0), axis=1, keepdims=True)
+            norm = jnp.sqrt(norm + 1e-06)
+        mine = pltpu.roll(line, wrap(LANES - s * nvl, LANES), axis=1)
+        out[0:1, t * nvl:(t + 1) * nvl] = mine[0:1, :nvl] / norm
     arrived(parts.at[others], p_send.at[0])
     arrived(sums.at[others], s_send.at[0])
 
@@ -476,8 +461,7 @@
             pltpu.VMEM((1, kept // Q), I32),
             pltpu.VMEM((1, kept // Q), I32),
             pltpu.VMEM(val_sketch.shape, F32),
-            pltpu.VMEM((local_rows, kept), F32),
-            pltpu.VMEM((local_rows, LANES), F32),
+            pltpu.VMEM((max(row_block, LANES), LANES), F32),
             pltpu.VMEM((kept, kept), I32),
             pltpu.VMEM((Q, 8, kept), I32),
             pltpu.VMEM((keep // LANES, LANES), F32),

time: 71.9 us -> 71.3 us (level)
  no operation moved by 1% of the time
where the time goes in v8:
time: 71.3 us; the launch traced here: 71.2 us
  Pallas kernels  70 us (98%)
  local copies, waits for them, and re-layouts  1.19 us (2%)
    pallas_call x1, Pallas kernels, body(): pl.pallas_call(functools.partial(kernel, (S, C, E), 1.0 / (math.sqrt(in_w...  70 us

profile of v8, /device:TPU:0, one launch (start us, length us, event | category | flops | bytes accessed | tf_op | source)
XLA Modules:
  0.0 71.2 jit_solution(3066775921759154991)
XLA Ops:
  0.0 70.0 %scores.1 = f32[1,64]{1,0:T(1,128)} custom-call(bf16[4,512,512]{2,1,0:T(8,128)(2,1)} %act.1, bf16[4,512,512]{2,1,0:T(8,128)(2,1)} %grads.1, s32[2048,128]{1,0:T(8,128)} %bitcast.4, s32[1,128]{1,0:T(1,128)} %bitcast.5, s32[1,32]{1,0:T(1,128)} %bitcast.6, s32[1,32]{1,0:T(1,128)} %bitcast.7, f32[16,2048]{1,0:T(8,128)} %val_in.1), custom_call_target="tpu_custom_call" | custom-call | flops 6442450944 | bytes 4194304 | tf_op jit(solution)/shard_map/scores/pallas_call | solution.py:444
  70.0 1.2 %copy.9 = f32[1,64]{1,0:T(1,128)} copy(f32[1,64]{1,0:T(1,128)} %scores.1) | data formatting | bytes 512

commit v9 on v8

--- a/solution.py
+++ b/solution.py
@@ -16,7 +16,7 @@
 BITS = 16
 ROWS = 256
 WIDE = 512
-WINDOW = 6
+WINDOW = 8
 
 
 def log2(n):

time: 71.3 us -> 71.3 us (level)
  no operation moved by 1% of the time
where the time goes in v9:
time: 71.3 us; the launch traced here: 71.2 us
  Pallas kernels  70 us (98%)
  local copies, waits for them, and re-layouts  1.19 us (2%)
    pallas_call x1, Pallas kernels, body(): pl.pallas_call(functools.partial(kernel, (S, C, E), 1.0 / (math.sqrt(in_w...  70 us

profile of v9, /device:TPU:0, one launch (start us, length us, event | category | flops | bytes accessed | tf_op | source)
XLA Modules:
  0.0 71.2 jit_solution(7520968351765680362)
XLA Ops:
  0.0 70.0 %scores.1 = f32[1,64]{1,0:T(1,128)} custom-call(bf16[4,512,512]{2,1,0:T(8,128)(2,1)} %act.1, bf16[4,512,512]{2,1,0:T(8,128)(2,1)} %grads.1, s32[2048,128]{1,0:T(8,128)} %bitcast.4, s32[1,128]{1,0:T(1,128)} %bitcast.5, s32[1,32]{1,0:T(1,128)} %bitcast.6, s32[1,32]{1,0:T(1,128)} %bitcast.7, f32[16,2048]{1,0:T(8,128)} %val_in.1), custom_call_target="tpu_custom_call" | custom-call | flops 6442450944 | bytes 4194304 | tf_op jit(solution)/shard_map/scores/pallas_call | solution.py:444
  70.0 1.2 %copy.9 = f32[1,64]{1,0:T(1,128)} copy(f32[1,64]{1,0:T(1,128)} %scores.1) | data formatting | bytes 512
